TPU v7x, 32 devices: a whole 2x2x4 slice. The times are simulated.
32 devices in a mesh: pb: 8 (over z, core), kv: 4 (over y, x).
Axes of the slice: x: 2, y: 2, z: 4, core: 2. Of those that a mesh axis runs over, the one named last changes fastest.
Arguments:
- queries: bfloat16 [49152, 1024], P(('pb', 'kv')), may hold values from -8 to 8
- keys: bfloat16 [65536, 128], P(('kv', 'pb')), may hold values from -6 to 6
- values: bfloat16 [65536, 128], P(('kv', 'pb')), may hold values from -6 to 6
- selected: int32 [768, 14], P(('pb', 'kv')), may hold values from 1 to 1022, as said below
Outputs:
- attended: bfloat16 [49152, 1024], P(('pb', 'kv'))
Inputs may be any that keep to these rules, and one draw needn't show every extreme that they name: `selected`: each row names 14 different blocks, never block 0 or block 1023. Key device k holds blocks k * 32 to (k + 1) * 32 - 1, devices counted with kv slowest; query device d holds query blocks d * 24 to (d + 1) * 24 - 1, devices counted with pb slowest. The query blocks of one device name together at most 2 distinct blocks of one key device, and in every draw some key device has exactly 2 named by every query device.
All inputs are finite; a program needn't handle non-finite values.
Results may differ from a plain program's by a relative error of at most 0.0046.
Values may be sent and summed in bfloat16 or wider, within the bound.
No kernel may reach another device: no remote copies, remote signals or barrier semaphores. Data moves between devices by JAX's collectives and lax.ppermute only.
A program may use at most 128 MiB of HBM per device.

v0:
```python
import math

import jax
import jax.numpy as jnp
from jax import lax
from jax.sharding import PartitionSpec as P

H = 8
DH = 128
BLOCK = 64
TOPN = 16
QB = 64
CAP = 2


def broadcast(value, axis, root):
    mine = lax.axis_index(axis) == root
    return lax.psum(jnp.where(mine, value, jnp.zeros_like(value)), axis)


def holdings(wanted, owner, blocks_here):
    local_ids = owner * blocks_here + jnp.arange(blocks_here, dtype=jnp.int32)
    hits = (wanted[:, None] == local_ids[None, :]).astype(jnp.int32)
    present = jnp.max(hits, axis=0)
    return (present, jnp.cumsum(present) - present)


def slot_lists(present, slot_rank, slots):
    local_ids = jnp.arange(present.shape[-1], dtype=jnp.int32)
    slot_ids = jnp.arange(slots, dtype=jnp.int32)
    matches = (present[..., :, None] == 1) & (slot_rank[..., :, None] == slot_ids)
    return jnp.sum(jnp.where(matches, local_ids[:, None], 0), axis=-2)


def per_device(queries, keys, values, selected):
    pb_count = lax.axis_size("pb")
    kv_count = lax.axis_size("kv")
    devices = pb_count * kv_count
    blocks_here = keys.shape[0] // BLOCK
    query_blocks = queries.shape[0] // QB
    tiles_local = jnp.concatenate(
        [keys.reshape(blocks_here, BLOCK, DH), values.reshape(blocks_here, BLOCK, DH)], axis=2
    )
    slots = CAP
    wanted = selected.reshape(-1)
    owners = jnp.arange(devices, dtype=jnp.int32)
    present, slot_rank = jax.vmap(lambda owner: holdings(wanted, owner, blocks_here))(owners)
    owner_lists = slot_lists(present, slot_rank, slots)
    by_axes = owner_lists.reshape(kv_count, pb_count, slots).transpose(1, 0, 2)
    asked_for = lax.all_to_all(
        lax.all_to_all(by_axes, "pb", split_axis=0, concat_axis=0, tiled=True),
        "kv",
        split_axis=1,
        concat_axis=1,
        tiled=True,
    )
    outgoing = jnp.take(tiles_local, asked_for.reshape(-1), axis=0).reshape(
        pb_count, kv_count, slots, BLOCK, 2 * DH
    )
    fetched = lax.all_to_all(
        lax.all_to_all(outgoing, "pb", split_axis=0, concat_axis=0, tiled=True),
        "kv",
        split_axis=1,
        concat_axis=1,
        tiled=True,
    )
    tile_table = fetched.reshape(devices * slots, BLOCK, 2 * DH)
    owner_of = selected // blocks_here
    positions = (owner_of % pb_count * kv_count + owner_of // pb_count) * slots + jnp.take(
        slot_rank.reshape(-1), selected
    )
    first_tile = broadcast(tiles_local[:1], ("pb", "kv"), 0)
    latest = broadcast(tiles_local[blocks_here - 1 :], ("pb", "kv"), devices - 1)
    tile_table = jnp.concatenate([tile_table, first_tile, latest], axis=0)
    extra_base = devices * slots
    leading_positions = jnp.broadcast_to(
        jnp.array([extra_base, extra_base + 1], jnp.int32), (query_blocks, 2)
    )
    positions = jnp.concatenate([leading_positions, positions], axis=1)
    group_size = math.gcd(query_blocks, 8)
    q_groups = queries.reshape(query_blocks // group_size, group_size, QB * H, DH)
    p_groups = positions.reshape(query_blocks // group_size, group_size, TOPN)

    def attend(operands):
        q_block, positions_in = operands
        gathered = jnp.take(tile_table, positions_in.reshape(-1), axis=0).reshape(
            group_size, TOPN * BLOCK, 2 * DH
        )
        scores = jnp.einsum(
            "gqd,gkd->gqk", q_block, gathered[..., :DH], preferred_element_type=jnp.float32
        ) * DH ** (-0.5)
        weights = jnp.exp(scores - jnp.max(scores, axis=-1, keepdims=True))
        totals = jnp.sum(weights, axis=-1, keepdims=True)
        weighted = jnp.einsum(
            "gqk,gkd->gqd",
            weights.astype(jnp.bfloat16),
            gathered[..., DH:],
            preferred_element_type=jnp.float32,
        )
        return (weighted / totals).astype(jnp.bfloat16)

    result = lax.map(attend, (q_groups, p_groups))
    return result.reshape(query_blocks * QB, H * DH)


def solution(mesh):
    placed = (
        P(("pb", "kv"), None),
        P(("kv", "pb"), None),
        P(("kv", "pb"), None),
        P(("pb", "kv"), None),
    )
    return jax.shard_map(
        per_device, mesh=mesh, in_specs=placed, out_specs=P(("pb", "kv"), None), check_vma=False
    )
```

profile of v0, /device:TPU:0, one launch (start us, length us, event | category | flops | bytes accessed | tf_op | source)
XLA Modules:
  0.0 288.0 jit_solution(515429109693339257)
XLA Ops:
  6.5 0.8 copy.42
  7.3 0.1 eq.47
  7.4 0.1 iota_add_fusion
  7.5 0.8 convert_reduce_fusion
  8.3 0.2 reduce_window_sum.11
  8.5 0.1 select_reduce_fusion
  8.6 0.1 reshape.151
  8.7 0.1 copy.49
  8.8 11.7 %all_to_all.20 = s32[8,4,2]{1,2,0:T(2,128)S(1)} all-to-all(s32[8,4,2]{1,2,0:T(2,128)S(1)} %copy.49), channel_id=1, replica_groups=mesh['pb'=8,'kv'=4] {'pb'}, dimensions={0} | all-to-all | bytes 512 | tf_op jit(solution)/shard_map/all_to_all | solution.py:51
  20.5 0.7 copy.50
  21.2 3.7 %all-to-all-start.1 = ((s32[8,4,2]{0,2,1:T(2,128)}), s32[8,4,2]{0,2,1:T(2,128)S(1)}, u32[]{:S(2)}, u32[]{:S(2)}) async-start(s32[8,4,2]{0,2,1:T(2,128)} %copy.50), calls=%async_computation.1 | async-start | bytes 8192 | tf_op jit(solution)/shard_map/all_to_all | solution.py:50
  24.9 1.3 pad_maximum_fusion.1
  26.2 3.3 %all-to-all-done.1 = s32[8,4,2]{0,2,1:T(2,128)S(1)} async-done(((s32[8,4,2]{0,2,1:T(2,128)}), s32[8,4,2]{0,2,1:T(2,128)S(1)}, u32[]{:S(2)}, u32[]{:S(2)}) %all-to-all-start.1) | async-done | bytes 288 | tf_op jit(solution)/shard_map/all_to_all | solution.py:50
  29.6 0.1 copy.52
  29.7 0.1 reshape.154
  29.8 0.1 copy.51
  30.0 0.7 gather_fusion.2
  30.6 0.3 broadcast_select_fusion
  30.9 51.5 %all_to_all.21 = bf16[8,4,2,64,256]{4,3,2,1,0:T(8,128)(2,1)S(1)} all-to-all(bf16[8,4,2,64,256]{4,3,2,1,0:T(8,128)(2,1)S(1)} %broadcast_select_fusion), channel_id=1, replica_groups=mesh['pb'=8,'kv'=4] {'pb'}, dimensions={0} | all-to-all | bytes 4194304 | tf_op jit(solution)/shard_map/all_to_all | solution.py:61
  82.4 1.5 copy.53
  83.9 3.7 %all-to-all-start.3 = ((bf16[8,4,2,64,256]{4,3,2,0,1:T(8,128)(2,1)}), bf16[8,4,2,64,256]{4,3,2,0,1:T(8,128)(2,1)S(1)}, u32[]{:S(2)}, u32[]{:S(2)}) async-start(bf16[8,4,2,64,256]{4,3,2,0,1:T(8,128)(2,1)} %copy.53), calls=%async_computation.3 | async-start | bytes 4194304 | tf_op jit(solution)/shard_map/all_to_all | solution.py:60
  87.7 0.0 all-reduce.3.cloned.1.call-start
  87.7 0.0 copy-done
  87.7 0.0 copy-done.1
  87.7 0.6 fusion.21
  88.4 0.0 all-reduce.3.cloned.1.call-update
  88.4 0.1 sub.32
  88.5 0.1 reshape.167
  88.6 0.0 copy-start.2
  88.6 1.9 gather_fusion.1
  90.5 0.1 reshape.166
  90.6 0.0 copy-done.2
  90.6 0.1 add_bitcast_fusion
  90.7 5.8 %reshape.149 = bf16[3,8,512,128]{3,2,1,0:T(8,128)(2,1)} reshape(bf16[1536,1024]{1,0:T(8,128)(2,1)} %param.7) | data formatting | bytes 6291456 | tf_op jit(solution)/shard_map/reshape | solution.py:81
  96.5 16.2 %all-to-all-done.3 = bf16[8,4,2,64,256]{4,3,2,0,1:T(8,128)(2,1)S(1)} async-done(((bf16[8,4,2,64,256]{4,3,2,0,1:T(8,128)(2,1)}), bf16[8,4,2,64,256]{4,3,2,0,1:T(8,128)(2,1)S(1)}, u32[]{:S(2)}, u32[]{:S(2)}) %all-to-all-start.3) | async-done | bytes 2097184 | tf_op jit(solution)/shard_map/all_to_all | solution.py:60
  112.7 1.5 copy.54
  114.2 102.0 %all-reduce.3.cloned.1.call-done = (bf16[1,64,256]{2,1,0:T(8,128)(2,1)}, bf16[1,64,256]{2,1,0:T(8,128)(2,1)}) async-done(((bf16[1,64,256]{2,1,0:T(8,128)(2,1)}, bf16[1,64,256]{2,1,0:T(8,128)(2,1)}), (bf16[1,64,256]{2,1,0:T(8,128)(2,1)}, bf16[1,64,256]{2,1,0:T(8,128)(2,1)})) %all-reduce.3.cloned.1.call-update) | async-done | bytes 65552 | tf_op jit(solution)/shard_map/psum | solution.py:18
  216.2 1.9 pad_maximum_fusion
  218.1 57.3 %while.10 = (s32[]{:T(128)}, bf16[3,8,512,128]{3,2,1,0:T(8,128)(2,1)}, bf16[3,8,512,128]{3,2,1,0:T(8,128)(2,1)}, s32[3,8,16]{2,1,0:T(8,128)S(1)}, bf16[66,64,256]{2,1,0:T(8,128)(2,1)S(1)}, /*index=5*/s32[]{:T(128)}) while((s32[]{:T(128)}, bf16[3,8,512,128]{3,2,1,0:T(8,128)(2,1)}, bf16[3,8,512,128]{3,2,1,0:T(8,128)(2,1)}, ...), condition=%wide.region_8.9_spmd, body=%wide.region_5.8_spmd.sunk | while | flops 2184177664 | bytes 73524552 | solution.py:102
  218.1 0.1 reshape.189
  218.2 2.7 gather_fusion
  221.0 0.1 broadcast_in_dim.84
  221.1 0.1 broadcast_in_dim.85
  221.2 4.6 %bitcast_select_fusion.2 = bf16[8,1024,256]{2,1,0:T(8,128)(2,1)S(1)} fusion(pred[8,1024]{1,0:T(8,128)(4,1)S(1)} %broadcast_in_dim.85, bf16[8,1024,256]{2,1,0:T(8,128)(2,1)} %bitcast.39), kind=kLoop, calls=%fused_computation.10.clone.1 | loop fusion | flops 2097152 | bytes 8396800 | tf_op jit(solution)/shard_map/while/body/eval_jaxpr/jit(_take)/select_n | solution.py:86
  225.7 3.6 %multiply_reduce_fusion.2 = (f32[8,512]{1,0:T(8,128)S(1)}, f32[8,512,1024]{2,1,0:T(8,128)S(1)}) fusion(bf16[8,1024,256]{2,1,0:T(8,128)(2,1)S(1)} %bitcast_select_fusion.2, bf16[3,8,512,128]{3,2,1,0:T(8,128)(2,1)} %get-tuple-element.104, s32[]{:T(128)} %get-tuple-element.96), kind=kOutput, calls=%fused_computation.4.clone.1 | convolution fusion | flops 1082126336 | bytes 19939840 | tf_op jit(solution)/shard_map/while/body/eval_jaxpr/gqd,gkd->gqk/dot_general | solution.py:89
  229.4 3.5 %fusion.41 = f32[8,512]{1,0:T(8,128)S(1)} fusion(f32[8,512,1024]{2,1,0:T(8,128)S(1)} %get-tuple-element.88, f32[8,512]{1,0:T(8,128)S(1)} %get-tuple-element.89), kind=kLoop, calls=%fused_computation.5.clone.1 | loop fusion | flops 12578816 | bytes 16809984 | tf_op jit(solution)/shard_map/while/body/eval_jaxpr/reduce_sum | solution.py:93
  232.9 4.3 %bitcast_dynamic-update-slice_fusion.2 = bf16[3,8,512,128]{3,2,1,0:T(8,128)(2,1)} fusion(bf16[3,8,512,128]{3,2,1,0:T(8,128)(2,1)} %get-tuple-element.97, s32[]{:T(128)} %get-tuple-element.96, f32[8,512]{1,0:T(8,128)S(1)} %fusion.41, bf16[8,1024,256]{2,1,0:T(8,128)(2,1)S(1)} %bitcast_select_fusion.2, f32[8,512,1024]{2,1,0:T(8,128)S(1)} %get-tuple-element.88, ...), kind=kOutput, calls=%fused_computation.15.clone.1 | convolution fusion | flops 1087373312 | bytes 19956224 | tf_op jit(solution)/shard_map/while/body/eval_jaxpr/gqk,gkd->gqd/dot_general | solution.py:94
  237.2 0.1 reshape.189
  237.3 2.7 gather_fusion
  240.1 0.1 broadcast_in_dim.84
  240.1 0.1 broadcast_in_dim.85
  240.2 4.6 %bitcast_select_fusion.2 = bf16[8,1024,256]{2,1,0:T(8,128)(2,1)S(1)} fusion(pred[8,1024]{1,0:T(8,128)(4,1)S(1)} %broadcast_in_dim.85, bf16[8,1024,256]{2,1,0:T(8,128)(2,1)} %bitcast.39), kind=kLoop, calls=%fused_computation.10.clone.1 | loop fusion | flops 2097152 | bytes 8396800 | tf_op jit(solution)/shard_map/while/body/eval_jaxpr/jit(_take)/select_n | solution.py:86
  244.8 3.6 %multiply_reduce_fusion.2 = (f32[8,512]{1,0:T(8,128)S(1)}, f32[8,512,1024]{2,1,0:T(8,128)S(1)}) fusion(bf16[8,1024,256]{2,1,0:T(8,128)(2,1)S(1)} %bitcast_select_fusion.2, bf16[3,8,512,128]{3,2,1,0:T(8,128)(2,1)} %get-tuple-element.104, s32[]{:T(128)} %get-tuple-element.96), kind=kOutput, calls=%fused_computation.4.clone.1 | convolution fusion | flops 1082126336 | bytes 19939840 | tf_op jit(solution)/shard_map/while/body/eval_jaxpr/gqd,gkd->gqk/dot_general | solution.py:89
  248.5 3.5 %fusion.41 = f32[8,512]{1,0:T(8,128)S(1)} fusion(f32[8,512,1024]{2,1,0:T(8,128)S(1)} %get-tuple-element.88, f32[8,512]{1,0:T(8,128)S(1)} %get-tuple-element.89), kind=kLoop, calls=%fused_computation.5.clone.1 | loop fusion | flops 12578816 | bytes 16809984 | tf_op jit(solution)/shard_map/while/body/eval_jaxpr/reduce_sum | solution.py:93
  252.0 4.3 %bitcast_dynamic-update-slice_fusion.2 = bf16[3,8,512,128]{3,2,1,0:T(8,128)(2,1)} fusion(bf16[3,8,512,128]{3,2,1,0:T(8,128)(2,1)} %get-tuple-element.97, s32[]{:T(128)} %get-tuple-element.96, f32[8,512]{1,0:T(8,128)S(1)} %fusion.41, bf16[8,1024,256]{2,1,0:T(8,128)(2,1)S(1)} %bitcast_select_fusion.2, f32[8,512,1024]{2,1,0:T(8,128)S(1)} %get-tuple-element.88, ...), kind=kOutput, calls=%fused_computation.15.clone.1 | convolution fusion | flops 1087373312 | bytes 19956224 | tf_op jit(solution)/shard_map/while/body/eval_jaxpr/gqk,gkd->gqd/dot_general | solution.py:94
  256.3 0.1 reshape.189
  256.4 2.7 gather_fusion
  259.1 0.1 broadcast_in_dim.84
  259.2 0.1 broadcast_in_dim.85
  259.3 4.6 %bitcast_select_fusion.2 = bf16[8,1024,256]{2,1,0:T(8,128)(2,1)S(1)} fusion(pred[8,1024]{1,0:T(8,128)(4,1)S(1)} %broadcast_in_dim.85, bf16[8,1024,256]{2,1,0:T(8,128)(2,1)} %bitcast.39), kind=kLoop, calls=%fused_computation.10.clone.1 | loop fusion | flops 2097152 | bytes 8396800 | tf_op jit(solution)/shard_map/while/body/eval_jaxpr/jit(_take)/select_n | solution.py:86
  263.9 3.6 %multiply_reduce_fusion.2 = (f32[8,512]{1,0:T(8,128)S(1)}, f32[8,512,1024]{2,1,0:T(8,128)S(1)}) fusion(bf16[8,1024,256]{2,1,0:T(8,128)(2,1)S(1)} %bitcast_select_fusion.2, bf16[3,8,512,128]{3,2,1,0:T(8,128)(2,1)} %get-tuple-element.104, s32[]{:T(128)} %get-tuple-element.96), kind=kOutput, calls=%fused_computation.4.clone.1 | convolution fusion | flops 1082126336 | bytes 19939840 | tf_op jit(solution)/shard_map/while/body/eval_jaxpr/gqd,gkd->gqk/dot_general | solution.py:89
  267.5 3.5 %fusion.41 = f32[8,512]{1,0:T(8,128)S(1)} fusion(f32[8,512,1024]{2,1,0:T(8,128)S(1)} %get-tuple-element.88, f32[8,512]{1,0:T(8,128)S(1)} %get-tuple-element.89), kind=kLoop, calls=%fused_computation.5.clone.1 | loop fusion | flops 12578816 | bytes 16809984 | tf_op jit(solution)/shard_map/while/body/eval_jaxpr/reduce_sum | solution.py:93
  271.1 4.3 %bitcast_dynamic-update-slice_fusion.2 = bf16[3,8,512,128]{3,2,1,0:T(8,128)(2,1)} fusion(bf16[3,8,512,128]{3,2,1,0:T(8,128)(2,1)} %get-tuple-element.97, s32[]{:T(128)} %get-tuple-element.96, f32[8,512]{1,0:T(8,128)S(1)} %fusion.41, bf16[8,1024,256]{2,1,0:T(8,128)(2,1)S(1)} %bitcast_select_fusion.2, f32[8,512,1024]{2,1,0:T(8,128)S(1)} %get-tuple-element.88, ...), kind=kOutput, calls=%fused_computation.15.clone.1 | convolution fusion | flops 1087373312 | bytes 19956224 | tf_op jit(solution)/shard_map/while/body/eval_jaxpr/gqk,gkd->gqd/dot_general | solution.py:94
  275.4 5.8 %reshape.156 = bf16[1536,1024]{1,0:T(8,128)(2,1)} reshape(bf16[3,8,512,128]{3,2,1,0:T(8,128)(2,1)} %get-tuple-element.32) | data formatting | bytes 6291456 | tf_op jit(solution)/shard_map/reshape | solution.py:103
  (22 shorter events, 0.2 us)
Async XLA Ops:
  21.2 8.4 %all-to-all-start.1 = ((s32[8,4,2]{0,2,1:T(2,128)}), s32[8,4,2]{0,2,1:T(2,128)S(1)}, u32[]{:S(2)}, u32[]{:S(2)}) async-start(s32[8,4,2]{0,2,1:T(2,128)} %copy.50), calls=%async_computation.1 | async-start | bytes 8192 | tf_op jit(solution)/shard_map/all_to_all | solution.py:50
  83.9 3.8 %copy-start = (bf16[2048,128]{1,0:T(8,128)(2,1)S(1)}, bf16[2048,128]{1,0:T(8,128)(2,1)}, u32[]{:S(2)}) copy-start(bf16[2048,128]{1,0:T(8,128)(2,1)} %param.9) | copy-start | bytes 1572868
  83.9 3.8 %copy-start.1 = (bf16[2048,128]{1,0:T(8,128)(2,1)S(1)}, bf16[2048,128]{1,0:T(8,128)(2,1)}, u32[]{:S(2)}) copy-start(bf16[2048,128]{1,0:T(8,128)(2,1)} %param.8) | copy-start | bytes 1572868
  83.9 28.8 %all-to-all-start.3 = ((bf16[8,4,2,64,256]{4,3,2,0,1:T(8,128)(2,1)}), bf16[8,4,2,64,256]{4,3,2,0,1:T(8,128)(2,1)S(1)}, u32[]{:S(2)}, u32[]{:S(2)}) async-start(bf16[8,4,2,64,256]{4,3,2,0,1:T(8,128)(2,1)} %copy.53), calls=%async_computation.3 | async-start | bytes 4194304 | tf_op jit(solution)/shard_map/all_to_all | solution.py:60
  87.7 128.5 %all-reduce.3.cloned.1.call-start = ((), (), s32[]{:S(2)}) async-start(), calls=%async_computation.4 | async-start | bytes 131072 | tf_op jit(solution)/shard_map/psum | solution.py:18
  88.6 2.0 copy-start.2
Sparse Core Ops, SparseCore 0:
  94.2 121.9 all-reduce.2
where the time goes:
time: 290 us; the launch traced here: 288 us
  waiting for transfers between devices  122 us (42%)
  blocking collectives  63.2 us (22%)
  other arithmetic  29.9 us (10%)
  local copies, waits for them, and re-layouts  28.4 us (10%)
  matrix products  23.7 us (8%)
  between operations  13.6 us (5%)
  starting transfers between devices  7.5 us (3%)
    psum x1, waiting for transfers between devices, broadcast(): return lax.psum(jnp.where(mine, value, jnp.zeros_like(value)), axis)  102 us
    all_to_all x1, blocking collectives, per_device(): lax.all_to_all(outgoing, 'pb', split_axis=0, concat_axis=0, tiled=True)  51.5 us
    all_to_all x1, waiting for transfers between devices, per_device(): lax.all_to_all(lax.all_to_all(outgoing, 'pb', split_axis=0, concat_axis=0...  16.2 us
    select_n x6, other arithmetic, attend(): jnp.take(tile_table, positions_in.reshape(-1), axis=0)  13.8 us
    dot_general x3, matrix products, attend(): jnp.einsum('gqk,gkd->gqd', weights.astype(jnp.bfloat16), gathered[..., DH...  12.8 us
    all_to_all x1, blocking collectives, per_device(): lax.all_to_all(by_axes, 'pb', split_axis=0, concat_axis=0, tiled=True)  11.7 us
    dot_general x3, matrix products, attend(): jnp.einsum('gqd,gkd->gqk', q_block, gathered[..., :DH], preferred_element...  10.9 us
    reduce_sum x3, other arithmetic, attend(): totals = jnp.sum(weights, axis=-1, keepdims=True)  10.6 us
  transfers between devices with their start and end apart: 3, of which 3 were waited for; matrix products, arithmetic and copies ran while one was open for 4% of the time, Pallas kernels for 0%

commit v1 on v0

v1 whole, which is shorter than its diff:
```python
import functools
import math

import jax
import jax.numpy as jnp
from jax import lax
from jax.experimental import pallas as pl
from jax.experimental.pallas import tpu as pltpu
from jax.sharding import Mesh
from jax.sharding import PartitionSpec as P

H = 8
DH = 128
BLOCK = 64
FREE = 14
QB = 64
CAP = 2
SCALE = DH ** -0.5 * math.log2(math.e)
HALF = ("pl", "kv")
ALL = ("hz", "pl", "kv")


def exchange(array, axes):
    return lax.all_to_all(array, axes, split_axis=0, concat_axis=0, tiled=True)


def attend(per_step, codes, q_ref, k_ref, near_ref, far_ref, forced_ref, out_ref):
    ones = jnp.ones((4 * BLOCK, DH), jnp.bfloat16)
    step = pl.program_id(0)
    for n in range(per_step):
        rows = q_ref[n * QB : (n + 1) * QB, :]
        stacked = jnp.concatenate([rows[:, h * DH : (h + 1) * DH] for h in range(H)], axis=0)
        key_tiles = [forced_ref[0, :BLOCK, :], forced_ref[1, :BLOCK, :]]
        value_tiles = [forced_ref[0, BLOCK:, :], forced_ref[1, BLOCK:, :]]
        for i in range(FREE):
            code = codes[(step * per_step + n) * FREE + i]
            source, slot = code // 4, code % 4
            key_tiles.append(k_ref[source, pl.ds(pl.multiple_of(slot * BLOCK, BLOCK), BLOCK), :])
            is_far = slot // 2
            second = slot % 2
            far = far_ref[source, second]
            near = near_ref[source, 2 + second]
            value_tiles.append(jnp.where(is_far == 1, far, near))
        key_groups = [jnp.concatenate(key_tiles[g * 4 : g * 4 + 4], axis=0) for g in range(4)]
        value_groups = [
            jnp.concatenate([jnp.concatenate(value_tiles[g * 4 : g * 4 + 4], axis=0), ones], axis=1)
            for g in range(4)
        ]
        for r in range(4):
            part = stacked[r * 128 : (r + 1) * 128]
            scores = [
                lax.dot_general(
                    part, k, (((1,), (1,)), ((), ())), preferred_element_type=jnp.float32
                )
                for k in key_groups
            ]
            top = functools.reduce(jnp.maximum, scores)
            top = jnp.max(top, axis=1, keepdims=True)
            total = None
            for s, v in zip(scores, value_groups):
                weights = jnp.exp2((s - top) * SCALE).astype(jnp.bfloat16)
                product = jnp.dot(weights, v, preferred_element_type=jnp.float32)
                total = product if total is None else total + product
            done = (total[:, :DH] / total[:, DH:]).astype(jnp.bfloat16)
            for i in range(2):
                h = r * 2 + i
                out_ref[n * QB : (n + 1) * QB, h * DH : (h + 1) * DH] = done[i * QB : (i + 1) * QB]


def per_device(queries, keys, values, selected):
    half_count = lax.axis_size("pl") * lax.axis_size("kv")
    kv_count = lax.axis_size("kv")
    pb_count = 2 * lax.axis_size("pl")
    devices = 2 * half_count
    blocks_here = keys.shape[0] // BLOCK
    query_blocks = queries.shape[0] // QB
    my_half = lax.axis_index("hz")
    me = lax.axis_index(ALL)
    swap = [(0, 1), (1, 0)]

    key_tiles = keys.reshape(blocks_here, BLOCK, DH)
    value_tiles = values.reshape(blocks_here, BLOCK, DH)
    far_keys = lax.ppermute(keys, "hz", swap).reshape(blocks_here, BLOCK, DH)

    flat = selected.reshape(-1)
    owner = flat // blocks_here
    local = flat % blocks_here
    place = owner % pb_count * kv_count + owner // pb_count
    second = jnp.any(
        (owner[:, None] == owner[None, :]) & (flat[None, :] < flat[:, None]), axis=1
    ).astype(jnp.int32)
    hit = place[None, :] == jnp.arange(devices, dtype=jnp.int32)[:, None]
    low = jnp.min(jnp.where(hit, local[None, :], blocks_here - 1), axis=1)
    high = jnp.max(jnp.where(hit, local[None, :], 0), axis=1)
    pairs = jnp.stack([low, high], axis=1).reshape(2, half_count, 2)
    wants = jnp.concatenate([pairs, pairs[::-1]], axis=2).reshape(devices, 4)
    codes = place % half_count * 4 + (place // half_count != my_half).astype(jnp.int32) * 2 + second

    piece = 2 * BLOCK // half_count
    edge = jnp.where(
        me == 0,
        jnp.concatenate([keys[:BLOCK], values[:BLOCK]], axis=0),
        jnp.concatenate([keys[-BLOCK:], values[-BLOCK:]], axis=0),
    ).reshape(half_count, piece, DH)
    header = jnp.pad(wants.astype(jnp.bfloat16)[:, None, :], ((0, 0), (0, 7), (0, DH - 4)))
    message = jnp.concatenate([header, jnp.concatenate([edge, edge], axis=0)], axis=1)
    answer = exchange(message, ALL)
    asked = answer[:, 0, :4].astype(jnp.int32).reshape(2, half_count, 4)
    asked_mine = jnp.where(my_half == 0, asked[0], asked[1])
    asked_other = jnp.where(my_half == 0, asked[1], asked[0])
    pieces = jnp.concatenate([answer[0, 8:], answer[devices - 1, 8:]], axis=0)

    wanted_values = jnp.concatenate([asked_other[:, :2], asked_mine[:, :2]], axis=1)
    value_parcel = jnp.take(value_tiles, wanted_values.reshape(-1), axis=0).reshape(
        half_count, 4, BLOCK, DH
    )
    near_values = exchange(value_parcel, HALF)
    far_values = lax.ppermute(near_values[:, :2], "hz", swap)

    near_keys = jnp.take(key_tiles, asked_mine[:, :2].reshape(-1), axis=0)
    passed_keys = jnp.take(far_keys, asked_mine[:, 2:].reshape(-1), axis=0)
    key_parcel = jnp.concatenate(
        [
            near_keys.reshape(half_count, 2 * BLOCK, DH),
            passed_keys.reshape(half_count, 2 * BLOCK, DH),
            jnp.broadcast_to(pieces[None], (half_count, 2 * piece, DH)),
        ],
        axis=1,
    )
    key_table = exchange(key_parcel, HALF)
    forced = (
        key_table[:, 4 * BLOCK :]
        .reshape(half_count, 2, piece, DH)
        .transpose(1, 0, 2, 3)
        .reshape(2, 2 * BLOCK, DH)
    )

    per_step = math.gcd(query_blocks, 4)
    whole = lambda shape: pl.BlockSpec(shape, lambda i, c: (0,) * len(shape))
    return pl.pallas_call(
        functools.partial(attend, per_step),
        out_shape=jax.ShapeDtypeStruct(queries.shape, queries.dtype),
        grid_spec=pltpu.PrefetchScalarGridSpec(
            num_scalar_prefetch=1,
            grid=(query_blocks // per_step,),
            in_specs=[
                pl.BlockSpec((per_step * QB, H * DH), lambda i, c: (i, 0)),
                whole(key_table.shape),
                whole(near_values.shape),
                whole(far_values.shape),
                whole(forced.shape),
            ],
            out_specs=pl.BlockSpec((per_step * QB, H * DH), lambda i, c: (i, 0)),
        ),
        compiler_params=pltpu.CompilerParams(vmem_limit_bytes=56 << 20),
    )(codes, queries, key_table, near_values, far_values, forced)


def solution(mesh):
    pb_count, kv_count = mesh.shape["pb"], mesh.shape["kv"]
    split = Mesh(mesh.devices.reshape(2, pb_count // 2, kv_count), ALL)
    by_query = P(("hz", "pl", "kv"), None)
    by_key = P(("kv", "hz", "pl"), None)
    return jax.shard_map(
        per_device,
        mesh=split,
        in_specs=(by_query, by_key, by_key, by_query),
        out_specs=by_query,
        check_vma=False,
    )
```

time: 290 us -> 107 us (0.37)
  waiting for transfers between devices: 122 us -> 54.9 us
  blocking collectives: 63.2 us -> 0 us
  other arithmetic: 29.9 us -> 4.28 us
  matrix products: 23.7 us -> 0 us
  Pallas kernels: 0 us -> 21.6 us
  local copies, waits for them, and re-layouts: 28.4 us -> 7.15 us
  between operations: 13.6 us -> 0.24 us
  starting transfers between devices: 7.5 us -> 18.3 us
    psum x1 -> x0, waiting for transfers between devices: 102 us -> none  [broadcast(): return lax.psum(jnp.where(mine, value, jnp.zeros_like(value)), axis)]
    all_to_all x2 -> x0, blocking collectives: 63.2 us -> none  [the longest x1 51.5 us: per_device(): lax.all_to_all(outgoing, 'pb', split_axis=0, concat_axis=0, tiled=True)]
    all_to_all x2 -> x3, waiting for transfers between devices: 19.5 us -> 51.6 us  [exchange(): return lax.all_to_all(array, axes, split_axis=0, concat_axis=0, tiled=True)]
    dot_general x6 -> x0, matrix products: 23.7 us -> none  [the longest x3 12.8 us: attend(): jnp.einsum('gqk,gkd->gqd', weights.astype(jnp.bfloat16), gathered[..., DH...]
    pallas_call x0 -> x1, Pallas kernels: none -> 21.6 us  [per_device(): pl.pallas_call(functools.partial(attend, per_step), out_shape=jax.ShapeDt...]
    select_n x10 -> x9, other arithmetic: 14.7 us -> 1.42 us  [the longest x2 1.14 us: per_device(): jnp.take(value_tiles, wanted_values.reshape(-1), axis=0)]
    reshape x7 -> x5, local copies, waits for them, and re-layouts: 12 us -> 1.01 us  [the longest x1 0.66 us: per_device(): forced = key_table[:, 4 * BLOCK:].reshape(half_count, 2, piece, DH).trans...]
    reduce_sum x4 -> x0, other arithmetic: 10.7 us -> none  [the longest x3 10.6 us: attend(): totals = jnp.sum(weights, axis=-1, keepdims=True)]
  transfers between devices with their start and end apart: 3 -> 5, of which waited for: 3 -> 4; matrix products, arithmetic and copies ran while one was open for 4% -> 6% of each run, Pallas kernels for 0% -> 0%
where the time goes in v1:
time: 107 us; the launch traced here: 106 us
  waiting for transfers between devices  54.9 us (51%)
  Pallas kernels  21.6 us (20%)
  starting transfers between devices  18.3 us (17%)
  local copies, waits for them, and re-layouts  7.15 us (7%)
  other arithmetic  4.28 us (4%)
    all_to_all x3, waiting for transfers between devices, exchange(): return lax.all_to_all(array, axes, split_axis=0, concat_axis=0, tiled=True)  51.6 us
    pallas_call x1, Pallas kernels, per_device(): pl.pallas_call(functools.partial(attend, per_step), out_shape=jax.ShapeDt...  21.6 us
    all_to_all x3, starting transfers between devices, exchange(): return lax.all_to_all(array, axes, split_axis=0, concat_axis=0, tiled=True)  14.9 us
    ppermute x1, waiting for transfers between devices, per_device(): far_keys = lax.ppermute(keys, 'hz', swap).reshape(blocks_here, BLOCK, DH)  3.27 us
    ppermute x1, starting transfers between devices, per_device(): far_keys = lax.ppermute(keys, 'hz', swap).reshape(blocks_here, BLOCK, DH)  2.74 us
  transfers between devices with their start and end apart: 5, of which 4 were waited for; matrix products, arithmetic and copies ran while one was open for 6% of the time, Pallas kernels for 0%

profile of v1, /device:TPU:0, one launch (start us, length us, event | category | flops | bytes accessed | tf_op | source)
XLA Modules:
  0.0 106.4 jit_solution(9754832020321788207)
XLA Ops:
  0.0 0.0 copy-start.2
  0.0 0.8 copy.36
  0.8 0.1 reshape.258
  0.9 0.3 and_reduce_fusion
  1.2 0.6 fusion.7
  1.8 0.1 select_reduce_fusion.1
  1.9 0.1 stack.9
  2.0 0.1 stack.10
  2.2 0.1 concatenate.41
  2.3 0.1 copy.45
  2.4 0.7 fusion.17
  3.1 0.7 fusion.16
  3.9 0.7 fusion.1
  4.6 7.3 %all-to-all-start = ((bf16[32,16,128]{2,1,0:T(8,128)(2,1)}), bf16[32,16,128]{2,1,0:T(8,128)(2,1)S(1)}, u32[]{:S(2)}, u32[]{:S(2)}) async-start(bf16[32,16,128]{2,1,0:T(8,128)(2,1)} %fusion.1), calls=%async_computation | async-start | bytes 262144 | tf_op jit(solution)/shard_map/all_to_all | solution.py:24
  11.9 2.7 %collective-permute-start = (bf16[2048,128]{1,0:T(8,128)(2,1)}, bf16[2048,128]{1,0:T(8,128)(2,1)S(1)}, u32[]{:S(2)}, u32[]{:S(2)}) collective-permute-start(bf16[2048,128]{1,0:T(8,128)(2,1)} %param.7), channel_id=1, source_target_pairs={{0,16},{16,0},{1,17},{17,1},{2,18},{18,2},{3,19},{19,3},{4,20},{20... | collective-permute-start | bytes 1572872 | tf_op jit(solution)/shard_map/ppermute | solution.py:83
  14.6 15.5 %all-to-all-done = bf16[32,16,128]{2,1,0:T(8,128)(2,1)S(1)} async-done(((bf16[32,16,128]{2,1,0:T(8,128)(2,1)}), bf16[32,16,128]{2,1,0:T(8,128)(2,1)S(1)}, u32[]{:S(2)}, u32[]{:S(2)}) %all-to-all-start) | async-done | bytes 131104 | tf_op jit(solution)/shard_map/all_to_all | solution.py:24
  30.2 0.1 copy.41
  30.3 0.1 copy.38
  30.4 0.1 copy.39
  30.5 0.1 copy.42
  30.6 0.1 copy.43
  30.7 0.1 reshape.266
  30.8 0.1 reshape.260
  30.9 0.0 copy-done.2
  30.9 0.7 gather_fusion
  31.6 1.1 %broadcast_select_fusion = bf16[16,4,64,128]{3,2,1,0:T(8,128)(2,1)} fusion(bf16[16,4,64,128]{3,2,1,0:T(8,128)(2,1)S(1)} %bitcast.29, pred[16,4]{1,0:T(8,128)(4,1)S(1)} %copy.42), kind=kLoop, calls=%fused_computation.4 | loop fusion | flops 524288 | bytes 2097216 | tf_op jit(solution)/shard_map/jit(_take)/select_n | solution.py:114
  32.8 0.0 copy-start.3
  32.8 3.9 %all-to-all-start.2 = ((bf16[16,4,64,128]{3,2,1,0:T(8,128)(2,1)}), bf16[16,4,64,128]{3,2,1,0:T(8,128)(2,1)S(1)}, u32[]{:S(2)}, u32[]{:S(2)}) async-start(bf16[16,4,64,128]{3,2,1,0:T(8,128)(2,1)} %broadcast_select_fusion), calls=%async_computation.2 | async-start | bytes 2097152 | tf_op jit(solution)/shard_map/all_to_all | solution.py:24
  36.7 0.1 copy.40
  36.8 0.1 reshape.263
  36.9 0.0 copy-done.3
  36.9 0.6 gather_fusion.1
  37.6 0.1 broadcast_select_fusion.2
  37.7 3.3 %collective-permute-done = bf16[2048,128]{1,0:T(8,128)(2,1)S(1)} collective-permute-done((bf16[2048,128]{1,0:T(8,128)(2,1)}, bf16[2048,128]{1,0:T(8,128)(2,1)S(1)}, u32[]{:S(2)}, u32[]{:S(2)}) %collective-permute-start) | collective-permute-done | bytes 524320 | tf_op jit(solution)/shard_map/ppermute | solution.py:83
  41.0 0.6 gather_fusion.2
  41.7 0.1 broadcast_select_fusion.1
  41.8 1.1 %pad_maximum_fusion = bf16[16,272,128]{2,1,0:T(8,128)(2,1)} fusion(bf16[16,16,128]{2,1,0:T(8,128)(2,1)S(1)} %broadcast_in_dim.53, bf16[16,128,128]{2,1,0:T(8,128)(2,1)S(1)} %bitcast.32, bf16[16,128,128]{2,1,0:T(8,128)(2,1)S(1)} %bitcast.31), kind=kLoop, calls=%fused_computation.3 | loop fusion | flops 3342336 | bytes 2228224 | tf_op jit(solution)/shard_map/concatenate | solution.py:122
  42.9 10.1 %all-to-all-done.2.near_ref = bf16[16,4,64,128]{3,2,1,0:T(8,128)(2,1)S(1)} async-done(((bf16[16,4,64,128]{3,2,1,0:T(8,128)(2,1)}), bf16[16,4,64,128]{3,2,1,0:T(8,128)(2,1)S(1)}, u32[]{:S(2)}, u32[]{:S(2)}) %all-to-all-start.2) | async-done | bytes 1048608 | tf_op jit(solution)/shard_map/all_to_all | solution.py:24
  53.0 0.0 copy-start
  53.0 3.7 %all-to-all-start.1 = ((bf16[16,272,128]{2,1,0:T(8,128)(2,1)}), bf16[16,272,128]{2,1,0:T(8,128)(2,1)S(1)}, u32[]{:S(2)}, u32[]{:S(2)}) async-start(bf16[16,272,128]{2,1,0:T(8,128)(2,1)} %pad_maximum_fusion), calls=%async_computation.1 | async-start | bytes 2228224 | tf_op jit(solution)/shard_map/all_to_all | solution.py:24
  56.7 0.0 copy-done
  56.8 0.7 collective-permute-start.1
  57.4 26.0 %all-to-all-done.1.k_ref = bf16[16,272,128]{2,1,0:T(8,128)(2,1)S(1)} async-done(((bf16[16,272,128]{2,1,0:T(8,128)(2,1)}), bf16[16,272,128]{2,1,0:T(8,128)(2,1)S(1)}, u32[]{:S(2)}, u32[]{:S(2)}) %all-to-all-start.1) | async-done | bytes 1114144 | tf_op jit(solution)/shard_map/all_to_all | solution.py:24
  83.4 0.0 copy-start.1
  83.4 0.7 copy_bitcast_fusion.forced_ref
  84.0 0.0 collective-permute-done.1.far_ref
  84.1 0.0 copy-start.4
  84.1 0.4 copy-done.1
  84.4 0.5 copy-done.4
  84.9 21.6 %shard_map.46 = bf16[1536,1024]{1,0:T(8,128)(2,1)} custom-call(s32[336]{0:T(512)} %get-tuple-element.8.codes, bf16[1536,1024]{1,0:T(8,128)(2,1)} %q_ref.1, bf16[16,272,128]{2,1,0:T(8,128)(2,1)} %copy-done.1, bf16[16,4,64,128]{3,2,1,0:T(8,128)(2,1)} %copy-done, bf16[16,2,64,128]{3,2,1,0:T(8,128)(2,1)} %copy-done.4, ...), custom_call_target="tpu_custom_call" | custom-call | tf_op jit(solution)/shard_map/pallas_call | solution.py:140
  (25 shorter events, 0.3 us)
Async XLA Ops:
  0.0 30.9 %copy-start.2 = (bf16[2048,128]{1,0:T(8,128)(2,1)S(1)}, bf16[2048,128]{1,0:T(8,128)(2,1)}, u32[]{:S(2)}) copy-start(bf16[2048,128]{1,0:T(8,128)(2,1)} %param.8) | copy-start | bytes 1572868
  4.6 25.6 %all-to-all-start = ((bf16[32,16,128]{2,1,0:T(8,128)(2,1)}), bf16[32,16,128]{2,1,0:T(8,128)(2,1)S(1)}, u32[]{:S(2)}, u32[]{:S(2)}) async-start(bf16[32,16,128]{2,1,0:T(8,128)(2,1)} %fusion.1), calls=%async_computation | async-start | bytes 262144 | tf_op jit(solution)/shard_map/all_to_all | solution.py:24
  11.9 29.2 %collective-permute-start = (bf16[2048,128]{1,0:T(8,128)(2,1)}, bf16[2048,128]{1,0:T(8,128)(2,1)S(1)}, u32[]{:S(2)}, u32[]{:S(2)}) collective-permute-start(bf16[2048,128]{1,0:T(8,128)(2,1)} %param.7), channel_id=1, source_target_pairs={{0,16},{16,0},{1,17},{17,1},{2,18},{18,2},{3,19},{19,3},{4,20},{20... | collective-permute-start | bytes 1572872 | tf_op jit(solution)/shard_map/ppermute | solution.py:83
  32.8 4.2 %copy-start.3 = (bf16[2048,128]{1,0:T(8,128)(2,1)S(1)}, bf16[2048,128]{1,0:T(8,128)(2,1)}, u32[]{:S(2)}) copy-start(bf16[2048,128]{1,0:T(8,128)(2,1)} %param.7) | copy-start | bytes 1572868
  32.8 20.2 %all-to-all-start.2 = ((bf16[16,4,64,128]{3,2,1,0:T(8,128)(2,1)}), bf16[16,4,64,128]{3,2,1,0:T(8,128)(2,1)S(1)}, u32[]{:S(2)}, u32[]{:S(2)}) async-start(bf16[16,4,64,128]{3,2,1,0:T(8,128)(2,1)} %broadcast_select_fusion), calls=%async_computation.2 | async-start | bytes 2097152 | tf_op jit(solution)/shard_map/all_to_all | solution.py:24
  53.0 3.7 %copy-start = (bf16[16,4,64,128]{3,2,1,0:T(8,128)(2,1)}, bf16[16,4,64,128]{3,2,1,0:T(8,128)(2,1)S(1)}, u32[]{:S(2)}) copy-start(bf16[16,4,64,128]{3,2,1,0:T(8,128)(2,1)S(1)} %all-to-all-done.2.near_ref) | copy-start | bytes 3145732
  53.0 30.4 %all-to-all-start.1 = ((bf16[16,272,128]{2,1,0:T(8,128)(2,1)}), bf16[16,272,128]{2,1,0:T(8,128)(2,1)S(1)}, u32[]{:S(2)}, u32[]{:S(2)}) async-start(bf16[16,272,128]{2,1,0:T(8,128)(2,1)} %pad_maximum_fusion), calls=%async_computation.1 | async-start | bytes 2228224 | tf_op jit(solution)/shard_map/all_to_all | solution.py:24
  56.8 27.3 %collective-permute-start.1 = (bf16[16,2,64,128]{3,2,1,0:T(8,128)(2,1)S(1)}, bf16[16,2,64,128]{3,2,1,0:T(8,128)(2,1)S(1)}, u32[]{:S(2)}, u32[]{:S(2)}) collective-permute-start(bf16[16,2,64,128]{3,2,1,0:T(8,128)(2,1)S(1)} %slice.74), channel_id=1, source_target_pairs={{0,16},{16,0},{1,17},{17,1},{2,18},{18,2},{3,19},{19,3},{4,20},{20... | collective-permute-start | bytes 1572872 | tf_op jit(solution)/shard_map/ppermute | solution.py:118
  83.4 1.0 copy-start.1
  84.1 0.8 copy-start.4

commit v2 on v1

v2 whole, which is shorter than its diff:
```python
import functools
import math

import jax
import jax.numpy as jnp
from jax import lax
from jax.experimental import pallas as pl
from jax.experimental.pallas import tpu as pltpu
from jax.sharding import PartitionSpec as P

H = 8
DH = 128
BLOCK = 64
FREE = 14
QB = 64
CAP = 2
HEADER = 8
SCALE = DH ** -0.5 * math.log2(math.e)
ALL = ("pb", "kv")


def exchange(array):
    return lax.all_to_all(array, ALL, split_axis=0, concat_axis=0, tiled=True)


def attend(per_step, codes, q_ref, table_ref, forced_ref, out_ref):
    ones = jnp.ones((4 * BLOCK, DH), jnp.bfloat16)
    step = pl.program_id(0)
    for n in range(per_step):
        rows = q_ref[n * QB : (n + 1) * QB, :]
        stacked = jnp.concatenate([rows[:, h * DH : (h + 1) * DH] for h in range(H)], axis=0)
        key_tiles = [forced_ref[0, :BLOCK, :], forced_ref[1, :BLOCK, :]]
        value_tiles = [forced_ref[0, BLOCK:, :], forced_ref[1, BLOCK:, :]]
        for i in range(FREE):
            code = codes[(step * per_step + n) * FREE + i]
            source = code // CAP
            row = pl.multiple_of(code % CAP * BLOCK, BLOCK)
            key_tiles.append(table_ref[source, pl.ds(row, BLOCK), :])
            value_tiles.append(table_ref[source, pl.ds(row + CAP * BLOCK, BLOCK), :])
        key_groups = [jnp.concatenate(key_tiles[g * 4 : g * 4 + 4], axis=0) for g in range(4)]
        value_groups = [
            jnp.concatenate([jnp.concatenate(value_tiles[g * 4 : g * 4 + 4], axis=0), ones], axis=1)
            for g in range(4)
        ]
        for r in range(4):
            part = stacked[r * 128 : (r + 1) * 128]
            scores = [
                lax.dot_general(
                    part, k, (((1,), (1,)), ((), ())), preferred_element_type=jnp.float32
                )
                for k in key_groups
            ]
            top = functools.reduce(jnp.maximum, scores)
            top = jnp.max(top, axis=1, keepdims=True)
            total = None
            for s, v in zip(scores, value_groups):
                weights = jnp.exp2((s - top) * SCALE).astype(jnp.bfloat16)
                product = jnp.dot(weights, v, preferred_element_type=jnp.float32)
                total = product if total is None else total + product
            done = (total[:, :DH] / total[:, DH:]).astype(jnp.bfloat16)
            for i in range(2):
                h = r * 2 + i
                out_ref[n * QB : (n + 1) * QB, h * DH : (h + 1) * DH] = done[i * QB : (i + 1) * QB]


def per_device(queries, keys, values, selected):
    pb_count = lax.axis_size("pb")
    kv_count = lax.axis_size("kv")
    devices = pb_count * kv_count
    blocks_here = keys.shape[0] // BLOCK
    query_blocks = queries.shape[0] // QB

    flat = selected.reshape(-1)
    owner = flat // blocks_here
    local = flat % blocks_here
    place = owner % pb_count * kv_count + owner // pb_count
    second = jnp.any(
        (owner[:, None] == owner[None, :]) & (flat[None, :] < flat[:, None]), axis=1
    ).astype(jnp.int32)
    codes = place * CAP + second
    hit = place[None, :] == jnp.arange(devices, dtype=jnp.int32)[:, None]
    low = jnp.min(jnp.where(hit, local[None, :], blocks_here - 1), axis=1)
    high = jnp.max(jnp.where(hit, local[None, :], 0), axis=1)
    wants = jnp.stack([low, high], axis=1).astype(jnp.bfloat16)

    span = 2 * BLOCK * DH // devices
    edges = jnp.stack(
        [
            jnp.concatenate([keys[:BLOCK], values[:BLOCK]], axis=0),
            jnp.concatenate([keys[-BLOCK:], values[-BLOCK:]], axis=0),
        ]
    ).reshape(2, devices, span)
    edges = edges.transpose(1, 0, 2).reshape(devices, 2 * span // DH, DH)
    header = jnp.pad(wants[:, None, :], ((0, 0), (0, HEADER - 1), (0, DH - CAP)))
    answer = exchange(jnp.concatenate([header, edges], axis=1))
    asked = answer[:, 0, :CAP].astype(jnp.int32)
    piece = jnp.concatenate(
        [answer[0, HEADER:].reshape(2, span)[:1], answer[devices - 1, HEADER:].reshape(2, span)[1:]]
    ).reshape(2 * span // DH, DH)

    def picked(array):
        tiles = jnp.take(array.reshape(blocks_here, BLOCK, DH), asked.reshape(-1), axis=0)
        return tiles.reshape(devices, CAP * BLOCK, DH)

    parcel = jnp.concatenate(
        [picked(keys), picked(values), jnp.broadcast_to(piece[None], (devices,) + piece.shape)],
        axis=1,
    )
    table = exchange(parcel)
    forced = (
        table[:, 2 * CAP * BLOCK :]
        .reshape(devices, 2, span)
        .transpose(1, 0, 2)
        .reshape(2, 2 * BLOCK, DH)
    )

    per_step = math.gcd(query_blocks, 4)
    whole = lambda shape: pl.BlockSpec(shape, lambda i, c: (0,) * len(shape))
    return pl.pallas_call(
        functools.partial(attend, per_step),
        out_shape=jax.ShapeDtypeStruct(queries.shape, queries.dtype),
        grid_spec=pltpu.PrefetchScalarGridSpec(
            num_scalar_prefetch=1,
            grid=(query_blocks // per_step,),
            in_specs=[
                pl.BlockSpec((per_step * QB, H * DH), lambda i, c: (i, 0)),
                whole(table.shape),
                whole(forced.shape),
            ],
            out_specs=pl.BlockSpec((per_step * QB, H * DH), lambda i, c: (i, 0)),
        ),
        compiler_params=pltpu.CompilerParams(vmem_limit_bytes=56 << 20),
    )(codes, queries, table, forced)


def solution(mesh):
    by_query = P(("pb", "kv"), None)
    by_key = P(("kv", "pb"), None)
    return jax.shard_map(
        per_device,
        mesh=mesh,
        in_specs=(by_query, by_key, by_key, by_query),
        out_specs=by_query,
        check_vma=False,
    )
```

time: 107 us -> 100 us (0.935)
  blocking collectives: 0 us -> 69.2 us
  waiting for transfers between devices: 54.9 us -> 0 us
  starting transfers between devices: 18.3 us -> 0 us
  other arithmetic: 4.28 us -> 1.58 us
    all_to_all x0 -> x2, blocking collectives: none -> 69.2 us  [exchange(): return lax.all_to_all(array, ALL, split_axis=0, concat_axis=0, tiled=True)]
    all_to_all x3 -> x0, waiting for transfers between devices: 51.6 us -> none  [exchange(): return lax.all_to_all(array, axes, split_axis=0, concat_axis=0, tiled=True)]
    all_to_all x3 -> x0, starting transfers between devices: 14.9 us -> none  [exchange(): return lax.all_to_all(array, axes, split_axis=0, concat_axis=0, tiled=True)]
    ppermute x2 -> x0, starting transfers between devices: 3.39 us -> none  [the longest x1 2.74 us: per_device(): far_keys = lax.ppermute(keys, 'hz', swap).reshape(blocks_here, BLOCK, DH)]
    ppermute x2 -> x0, waiting for transfers between devices: 3.27 us -> none  [the longest x1 3.27 us: per_device(): far_keys = lax.ppermute(keys, 'hz', swap).reshape(blocks_here, BLOCK, DH)]
    concatenate x6 -> x4, other arithmetic: 1.79 us -> 0.23 us  [the longest x1 0.17 us: per_device(): jnp.concatenate([picked(keys), picked(values), jnp.broadcast_to(piece[Non...]
    select_n x8 -> x2, other arithmetic: 1.41 us -> 0.26 us  [picked(): jnp.take(array.reshape(blocks_here, BLOCK, DH), asked.reshape(-1), axis=0)]
    gather x3 -> x2, local copies, waits for them, and re-layouts: 2.04 us -> 2.54 us  [picked(): jnp.take(array.reshape(blocks_here, BLOCK, DH), asked.reshape(-1), axis=0)]
  transfers between devices with their start and end apart: 5 -> 0, of which waited for: 4 -> 0; matrix products, arithmetic and copies ran while one was open for 6% -> 0% of each run, Pallas kernels for 0% -> 0%
where the time goes in v2:
time: 100 us; the launch traced here: 99.5 us
  blocking collectives  69.2 us (69%)
  Pallas kernels  21.8 us (22%)
  local copies, waits for them, and re-layouts  6.73 us (7%)
  other arithmetic  1.58 us (2%)
    all_to_all x2, blocking collectives, exchange(): return lax.all_to_all(array, ALL, split_axis=0, concat_axis=0, tiled=True)  69.2 us
    pallas_call x1, Pallas kernels, per_device(): pl.pallas_call(functools.partial(attend, per_step), out_shape=jax.ShapeDt...  21.8 us
    gather x2, local copies, waits for them, and re-layouts, picked(): jnp.take(array.reshape(blocks_here, BLOCK, DH), asked.reshape(-1), axis=0)  2.54 us

profile of v2, /device:TPU:0, one launch (start us, length us, event | category | flops | bytes accessed | tf_op | source)
XLA Modules:
  0.0 99.5 jit_solution(10929834472717607451)
XLA Ops:
  0.0 0.0 copy-start.1
  0.0 0.8 copy.21
  0.8 0.1 reshape.191
  0.9 0.3 and_reduce_fusion
  1.2 0.6 convert_add_fusion
  1.8 0.1 select_reduce_fusion.1
  2.0 0.1 copy.25
  2.1 0.7 fusion.9
  2.8 0.7 fusion.10
  3.7 0.1 copy.22
  3.8 15.5 %all_to_all.10 = bf16[32,16,128]{2,1,0:T(8,128)(2,1)S(1)} all-to-all(bf16[32,16,128]{2,1,0:T(8,128)(2,1)S(1)} %fusion.1), channel_id=1, replica_groups=mesh['pb'=8,'kv'=4] {'pb','kv'}, dimensions={0} | all-to-all | bytes 262144 | tf_op jit(solution)/shard_map/all_to_all | solution.py:23
  19.3 0.1 fusion.2
  19.4 0.1 reshape.199
  19.6 1.8 %gather_fusion.1 = bf16[64,64,128]{2,1,0:T(8,128)(2,1)S(1)} fusion(bf16[32,64,128]{2,1,0:T(8,128)(2,1)} %bitcast.25, s32[1024]{0:T(1024)S(1)} %pad_clamp_fusion), kind=kCustom, calls=%fused_computation.1.clone | custom fusion | bytes 2097408 | tf_op jit(solution)/shard_map/jit(_take)/gather | solution.py:102
  21.4 0.0 copy-done.1
  21.4 0.7 gather_fusion
  22.2 0.3 broadcast_select_fusion.1
  22.5 0.2 pad_maximum_fusion
  22.6 53.7 %all_to_all.11.table_ref = bf16[32,264,128]{2,1,0:T(8,128)(2,1)S(1)} all-to-all(bf16[32,264,128]{2,1,0:T(8,128)(2,1)S(1)} %pad_maximum_fusion), channel_id=1, replica_groups=mesh['pb'=8,'kv'=4] {'pb','kv'}, dimensions={0} | all-to-all | bytes 4325376 | tf_op jit(solution)/shard_map/all_to_all | solution.py:23
  76.3 0.0 copy-start
  76.4 0.8 reshape.198.forced_ref
  77.2 0.5 copy-done
  77.7 21.8 %shard_map.46 = bf16[1536,1024]{1,0:T(8,128)(2,1)} custom-call(s32[336]{0:T(512)} %get-tuple-element.8.codes, bf16[1536,1024]{1,0:T(8,128)(2,1)} %q_ref.1, bf16[32,264,128]{2,1,0:T(8,128)(2,1)} %copy-done, bf16[2,128,128]{2,1,0:T(8,128)(2,1)} %reshape.198.forced_ref), custom_call_target="tpu_custom_call" | custom-call | tf_op jit(solution)/shard_map/pallas_call | solution.py:119
  (21 shorter events, 0.3 us)
Async XLA Ops:
  0.0 21.4 %copy-start.1 = (bf16[2048,128]{1,0:T(8,128)(2,1)S(1)}, bf16[2048,128]{1,0:T(8,128)(2,1)}, u32[]{:S(2)}) copy-start(bf16[2048,128]{1,0:T(8,128)(2,1)} %param.7) | copy-start | bytes 1572868
  76.3 1.4 %copy-start = (bf16[32,264,128]{2,1,0:T(8,128)(2,1)}, bf16[32,264,128]{2,1,0:T(8,128)(2,1)S(1)}, u32[]{:S(2)}) copy-start(bf16[32,264,128]{2,1,0:T(8,128)(2,1)S(1)} %all_to_all.11.table_ref) | copy-start | bytes 6488068

commit v3 on v2

v3 whole, which is shorter than its diff:
```python
import functools
import math

import jax
import jax.numpy as jnp
from jax import lax
from jax.experimental import pallas as pl
from jax.experimental.pallas import tpu as pltpu
from jax.sharding import PartitionSpec as P

H = 8
DH = 128
BLOCK = 64
FREE = 14
QB = 64
CAP = 2
PIECES = 32
PIECE = 4 * BLOCK // PIECES
CHUNK = 256
GROUP = 4
SCALE = DH ** -0.5 * math.log2(math.e)
ALL = ("pb", "kv")


def exchange(array):
    return lax.all_to_all(array, ALL, split_axis=0, concat_axis=0, tiled=True)


def prepare(devices, blocks_here, place_ref, local_ref, fk, fv, lk, lv, code_ref, message_ref):
    rows, columns = place_ref.shape
    ids = lax.broadcasted_iota(jnp.int32, (devices, columns), 0)
    low = jnp.full((devices, columns), blocks_here - 1, jnp.int32)
    high = jnp.zeros((devices, columns), jnp.int32)
    for r in range(rows):
        hit = place_ref[r : r + 1, :] == ids
        local = jnp.broadcast_to(local_ref[r : r + 1, :], ids.shape)
        low = jnp.where(hit, jnp.minimum(low, local), low)
        high = jnp.where(hit, jnp.maximum(high, local), high)
    low = jnp.min(low, axis=1, keepdims=True)
    high = jnp.max(high, axis=1, keepdims=True)
    for r in range(rows):
        place, local = place_ref[r : r + 1, :], local_ref[r : r + 1, :]
        above = jnp.where((place == ids) & (local > low), 1, 0)
        code_ref[r : r + 1, :] = place * CAP + jnp.max(above, axis=0, keepdims=True)
    lane = lax.broadcasted_iota(jnp.int32, (devices, DH), 1)
    wants = jnp.where(lane == 0, low, jnp.where(lane == 1, high, 0)).astype(jnp.float32)
    wants = jnp.broadcast_to(wants[:, None, :], (devices, PIECE, DH))
    message_ref[:, :PIECE, :] = wants.astype(jnp.bfloat16)
    edges = jnp.concatenate([fk[...], fv[...], lk[...], lv[...]], axis=0).astype(jnp.float32)
    edges = edges.reshape(PIECES, PIECE, DH).astype(jnp.bfloat16)
    for at in range(0, devices, PIECES):
        message_ref[at : at + PIECES, PIECE:, :] = edges


def pack(devices, asked, answer_ref, k_ref, v_ref, parcel_ref):
    late = asked[devices * CAP]
    piece = answer_ref[late * (devices - 1), PIECE:, :]

    @pl.loop(0, devices)
    def _(m):
        for slot in range(CAP):
            row = pl.multiple_of(asked[m * CAP + slot] * BLOCK, BLOCK)
            at = slot * BLOCK
            parcel_ref[m, at : at + BLOCK, :] = k_ref[pl.ds(row, BLOCK), :]
            at += CAP * BLOCK
            parcel_ref[m, at : at + BLOCK, :] = v_ref[pl.ds(row, BLOCK), :]
        parcel_ref[m, 2 * CAP * BLOCK :, :] = piece


def attend(per_step, codes, q_ref, table_ref, out_ref, edge_ref):
    step = pl.program_id(0)

    @pl.when(step == 0)
    def _():
        edges = table_ref[:PIECES, 2 * CAP * BLOCK :, :].astype(jnp.float32)
        edge_ref[...] = edges.reshape(4 * BLOCK, DH).astype(jnp.bfloat16)

    ones = jnp.ones((GROUP * BLOCK, DH), jnp.bfloat16)
    groups = (FREE + 2) // GROUP
    chunks = QB * H // CHUNK

    def load(n):
        rows = q_ref[n * QB : (n + 1) * QB, :]
        stacked = jnp.concatenate([rows[:, h * DH : (h + 1) * DH] for h in range(H)], axis=0)
        key_tiles = [edge_ref[:BLOCK, :], edge_ref[2 * BLOCK : 3 * BLOCK, :]]
        value_tiles = [edge_ref[BLOCK : 2 * BLOCK, :], edge_ref[3 * BLOCK :, :]]
        for i in range(FREE):
            code = codes[step * per_step + n, i]
            source = code // CAP
            row = pl.multiple_of(code % CAP * BLOCK, BLOCK)
            key_tiles.append(table_ref[source, pl.ds(row, BLOCK), :])
            value_tiles.append(table_ref[source, pl.ds(row + CAP * BLOCK, BLOCK), :])
        join = lambda tiles, g: jnp.concatenate(tiles[g * GROUP : (g + 1) * GROUP], axis=0)
        return (
            stacked,
            [join(key_tiles, g) for g in range(groups)],
            [jnp.concatenate([join(value_tiles, g), ones], axis=1) for g in range(groups)],
        )

    def score(block, c):
        part = block[0][c * CHUNK : (c + 1) * CHUNK]
        scores = [
            lax.dot_general(part, k, (((1,), (1,)), ((), ())), preferred_element_type=jnp.float32)
            for k in block[1]
        ]
        tops = [jnp.max(s, axis=1, keepdims=True) for s in scores]
        return scores, functools.reduce(jnp.maximum, tops)

    def finish(block, n, c, scores, top):
        total = None
        for s, v in zip(scores, block[2]):
            weights = jnp.exp2((s - top) * SCALE).astype(jnp.bfloat16)
            product = jnp.dot(weights, v, preferred_element_type=jnp.float32)
            total = product if total is None else total + product
        done = (total[:, :DH] / total[:, DH:]).astype(jnp.bfloat16)
        for i in range(CHUNK // QB):
            h = c * (CHUNK // QB) + i
            out_ref[n * QB : (n + 1) * QB, h * DH : (h + 1) * DH] = done[i * QB : (i + 1) * QB]

    waiting = None
    for n in range(per_step):
        block = load(n)
        for c in range(chunks):
            scored = (block, n, c, *score(block, c))
            if waiting is not None:
                finish(*waiting)
            waiting = scored
    finish(*waiting)


def per_device(queries, keys, values, selected):
    pb_count = lax.axis_size("pb")
    kv_count = lax.axis_size("kv")
    devices = pb_count * kv_count
    blocks_here = keys.shape[0] // BLOCK
    query_blocks = queries.shape[0] // QB

    owner = selected // blocks_here
    local = selected % blocks_here
    place = owner % pb_count * kv_count + owner // pb_count
    first = pl.BlockSpec((BLOCK, DH), lambda i: (0, 0))
    last = pl.BlockSpec((BLOCK, DH), lambda i: (blocks_here - 1, 0))
    held = pl.BlockSpec(selected.shape, lambda i: (0, 0))
    message_shape = (devices, 2 * PIECE, DH)
    codes, message = pl.pallas_call(
        functools.partial(prepare, devices, blocks_here),
        grid=(1,),
        in_specs=[held, held, first, first, last, last],
        out_specs=[held, pl.BlockSpec(message_shape, lambda i: (0, 0, 0))],
        out_shape=[
            jax.ShapeDtypeStruct(selected.shape, jnp.int32),
            jax.ShapeDtypeStruct(message_shape, jnp.bfloat16),
        ],
    )(place, local, keys, values, keys, values)

    answer = exchange(message)
    late = (lax.axis_index(ALL) % PIECES >= PIECES // 2).astype(jnp.int32)
    asked = jnp.concatenate([answer[:, 0, :CAP].astype(jnp.int32).reshape(-1), late[None]])
    parcel_shape = (devices, 2 * CAP * BLOCK + PIECE, DH)
    parcel_bytes = 2 * math.prod(parcel_shape)
    parcel = pl.pallas_call(
        functools.partial(pack, devices),
        grid_spec=pltpu.PrefetchScalarGridSpec(
            num_scalar_prefetch=1,
            grid=(),
            in_specs=[pl.BlockSpec(memory_space=pltpu.VMEM)] * 3,
            out_specs=pl.BlockSpec(memory_space=pltpu.VMEM),
        ),
        out_shape=jax.ShapeDtypeStruct(parcel_shape, keys.dtype),
        compiler_params=pltpu.CompilerParams(vmem_limit_bytes=(8 << 20) + parcel_bytes),
    )(asked, answer, keys, values)
    table = exchange(parcel)

    per_step = math.gcd(query_blocks, 6)
    return pl.pallas_call(
        functools.partial(attend, per_step),
        out_shape=jax.ShapeDtypeStruct(queries.shape, queries.dtype),
        grid_spec=pltpu.PrefetchScalarGridSpec(
            num_scalar_prefetch=1,
            grid=(query_blocks // per_step,),
            in_specs=[
                pl.BlockSpec((per_step * QB, H * DH), lambda i, c: (i, 0)),
                pl.BlockSpec(parcel_shape, lambda i, c: (0, 0, 0)),
            ],
            out_specs=pl.BlockSpec((per_step * QB, H * DH), lambda i, c: (i, 0)),
            scratch_shapes=[pltpu.VMEM((4 * BLOCK, DH), jnp.bfloat16)],
        ),
        compiler_params=pltpu.CompilerParams(vmem_limit_bytes=56 << 20),
    )(codes, queries, table)


def solution(mesh):
    by_query = P(("pb", "kv"), None)
    by_key = P(("kv", "pb"), None)
    return jax.shard_map(
        per_device,
        mesh=mesh,
        in_specs=(by_query, by_key, by_key, by_query),
        out_specs=by_query,
        check_vma=False,
    )
```

time: 100 us -> 96.8 us (0.968)
  blocking collectives: 69.2 us -> 54.3 us
  waiting for transfers between devices: 0 us -> 8.39 us
  starting transfers between devices: 0 us -> 7.3 us
  local copies, waits for them, and re-layouts: 6.73 us -> 2.96 us
    all_to_all x2 -> x1, blocking collectives: 69.2 us -> 54.3 us  [exchange(): return lax.all_to_all(array, ALL, split_axis=0, concat_axis=0, tiled=True)]
    all_to_all x0 -> x1, waiting for transfers between devices: none -> 8.39 us  [exchange(): return lax.all_to_all(array, ALL, split_axis=0, concat_axis=0, tiled=True)]
    all_to_all x0 -> x1, starting transfers between devices: none -> 7.3 us  [exchange(): return lax.all_to_all(array, ALL, split_axis=0, concat_axis=0, tiled=True)]
    pallas_call x0 -> x2, Pallas kernels: none -> 2.65 us  [the longest x1 1.77 us: per_device(): pl.pallas_call(functools.partial(prepare, devices, blocks_here), grid=(1,...]
    gather x2 -> x0, local copies, waits for them, and re-layouts: 2.54 us -> none  [picked(): jnp.take(array.reshape(blocks_here, BLOCK, DH), asked.reshape(-1), axis=0)]
    pallas_call x1, Pallas kernels: 21.8 us -> 19.8 us  [per_device(): pl.pallas_call(functools.partial(attend, per_step), out_shape=jax.ShapeDt...]
    slice x3 -> x0, local copies, waits for them, and re-layouts: 1.48 us -> none  [the longest x1 0.74 us: per_device(): keys[:BLOCK]]
    unnamed x9 -> x5, local copies, waits for them, and re-layouts: 1.48 us -> 2.86 us
  transfers between devices with their start and end apart: 0 -> 1, of which waited for: 0 -> 1; matrix products, arithmetic and copies ran while one was open for 0% -> 0% of each run, Pallas kernels for 0% -> 0%
where the time goes in v3:
time: 96.8 us; the launch traced here: 96.3 us
  blocking collectives  54.3 us (56%)
  Pallas kernels  22.5 us (23%)
  waiting for transfers between devices  8.39 us (9%)
  starting transfers between devices  7.3 us (8%)
  local copies, waits for them, and re-layouts  2.96 us (3%)
    all_to_all x1, blocking collectives, exchange(): return lax.all_to_all(array, ALL, split_axis=0, concat_axis=0, tiled=True)  54.3 us
    pallas_call x1, Pallas kernels, per_device(): pl.pallas_call(functools.partial(attend, per_step), out_shape=jax.ShapeDt...  19.8 us
    all_to_all x1, waiting for transfers between devices, exchange(): return lax.all_to_all(array, ALL, split_axis=0, concat_axis=0, tiled=True)  8.39 us
    all_to_all x1, starting transfers between devices, exchange(): return lax.all_to_all(array, ALL, split_axis=0, concat_axis=0, tiled=True)  7.3 us
    unnamed x5, local copies, waits for them, and re-layouts  2.86 us
  transfers between devices with their start and end apart: 1, of which 1 were waited for; matrix products, arithmetic and copies ran while one was open for 0% of the time, Pallas kernels for 0%

profile of v3, /device:TPU:0, one launch (start us, length us, event | category | flops | bytes accessed | tf_op | source)
XLA Modules:
  0.0 96.3 jit_solution(4919276326702001421)
XLA Ops:
  0.0 0.8 copy.9
  0.8 0.6 add_select_fusion
  1.4 1.8 %shard_map.46 = (s32[24,14]{1,0:T(8,128)}, bf16[32,16,128]{2,1,0:T(8,128)(2,1)}) custom-call(s32[24,14]{1,0:T(8,128)} %get-tuple-element.10.place_ref, s32[24,14]{1,0:T(8,128)} %get-tuple-element.9.local_ref, bf16[2048,128]{1,0:T(8,128)(2,1)} %k_ref.1, bf16[2048,128]{1,0:T(8,128)(2,1)} %v_ref.1, bf16[2048,128]{1,0:T(8,128)(2,1)} %k_ref.1, ...), custom_call_target="tpu_custom_call" | custom-call | tf_op jit(solution)/shard_map/pallas_call | solution.py:145
  3.2 7.3 %all-to-all-start = ((bf16[32,16,128]{2,1,0:T(8,128)(2,1)}), bf16[32,16,128]{2,1,0:T(8,128)(2,1)S(1)}, u32[]{:S(2)}, u32[]{:S(2)}) async-start(bf16[32,16,128]{2,1,0:T(8,128)(2,1)} %get-tuple-element.8), calls=%async_computation | async-start | bytes 262144 | tf_op jit(solution)/shard_map/all_to_all | solution.py:26
  10.5 8.4 %all-to-all-done.answer_ref = bf16[32,16,128]{2,1,0:T(8,128)(2,1)S(1)} async-done(((bf16[32,16,128]{2,1,0:T(8,128)(2,1)}), bf16[32,16,128]{2,1,0:T(8,128)(2,1)S(1)}, u32[]{:S(2)}, u32[]{:S(2)}) %all-to-all-start) | async-done | bytes 131104 | tf_op jit(solution)/shard_map/all_to_all | solution.py:26
  18.9 0.1 fusion
  18.9 0.1 reshape.4
  19.0 0.1 pad_add_fusion.asked
  19.1 0.0 copy-start
  19.1 1.0 %copy-done = bf16[2048,128]{1,0:T(8,128)(2,1)S(1)} copy-done((bf16[2048,128]{1,0:T(8,128)(2,1)S(1)}, bf16[2048,128]{1,0:T(8,128)(2,1)}, u32[]{:S(2)}) %copy-start) | copy-done | bytes 524312
  20.2 0.0 copy-start.1
  20.2 1.0 %copy-done.1 = bf16[2048,128]{1,0:T(8,128)(2,1)S(1)} copy-done((bf16[2048,128]{1,0:T(8,128)(2,1)S(1)}, bf16[2048,128]{1,0:T(8,128)(2,1)}, u32[]{:S(2)}) %copy-start.1) | copy-done | bytes 524312
  21.2 0.9 shard_map.47
  22.1 54.3 %all_to_all.10.table_ref = bf16[32,264,128]{2,1,0:T(8,128)(2,1)} all-to-all(bf16[32,264,128]{2,1,0:T(8,128)(2,1)S(1)} %shard_map.47), channel_id=1, replica_groups=mesh['pb'=8,'kv'=4] {'pb','kv'}, dimensions={0} | all-to-all | bytes 4325376 | tf_op jit(solution)/shard_map/all_to_all | solution.py:26
  76.4 19.8 %shard_map.48 = bf16[1536,1024]{1,0:T(8,128)(2,1)} custom-call(s32[24,14]{1,0:T(8,128)} %get-tuple-element.7.codes, bf16[1536,1024]{1,0:T(8,128)(2,1)} %q_ref.1, bf16[32,264,128]{2,1,0:T(8,128)(2,1)} %all_to_all.10.table_ref), custom_call_target="tpu_custom_call" | custom-call | tf_op jit(solution)/shard_map/pallas_call | solution.py:175
Async XLA Ops:
  3.2 15.7 %all-to-all-start = ((bf16[32,16,128]{2,1,0:T(8,128)(2,1)}), bf16[32,16,128]{2,1,0:T(8,128)(2,1)S(1)}, u32[]{:S(2)}, u32[]{:S(2)}) async-start(bf16[32,16,128]{2,1,0:T(8,128)(2,1)} %get-tuple-element.8), calls=%async_computation | async-start | bytes 262144 | tf_op jit(solution)/shard_map/all_to_all | solution.py:26
  19.1 1.0 %copy-start = (bf16[2048,128]{1,0:T(8,128)(2,1)S(1)}, bf16[2048,128]{1,0:T(8,128)(2,1)}, u32[]{:S(2)}) copy-start(bf16[2048,128]{1,0:T(8,128)(2,1)} %k_ref.1) | copy-start | bytes 1572868
  20.2 1.0 %copy-start.1 = (bf16[2048,128]{1,0:T(8,128)(2,1)S(1)}, bf16[2048,128]{1,0:T(8,128)(2,1)}, u32[]{:S(2)}) copy-start(bf16[2048,128]{1,0:T(8,128)(2,1)} %v_ref.1) | copy-start | bytes 1572868

commit v4 on v3

--- a/solution.py
+++ b/solution.py
@@ -26,20 +26,30 @@
     return lax.all_to_all(array, ALL, split_axis=0, concat_axis=0, tiled=True)
 
 
-def prepare(devices, blocks_here, place_ref, local_ref, fk, fv, lk, lv, code_ref, message_ref):
-    rows, columns = place_ref.shape
+def divide(array, n):
+    if n & (n - 1) == 0:
+        return array >> (n.bit_length() - 1), array & (n - 1)
+    return array // n, array % n
+
+
+def prepare(pb_count, kv_count, blocks_here, selected_ref, fk, fv, lk, lv, code_ref, message_ref):
+    devices = pb_count * kv_count
+    rows, columns = selected_ref.shape
+    owner, locals_ = divide(selected_ref[...], blocks_here)
+    owner_kv, owner_pb = divide(owner, pb_count)
+    places = owner_pb * kv_count + owner_kv
     ids = lax.broadcasted_iota(jnp.int32, (devices, columns), 0)
     low = jnp.full((devices, columns), blocks_here - 1, jnp.int32)
     high = jnp.zeros((devices, columns), jnp.int32)
     for r in range(rows):
-        hit = place_ref[r : r + 1, :] == ids
-        local = jnp.broadcast_to(local_ref[r : r + 1, :], ids.shape)
+        hit = places[r : r + 1, :] == ids
+        local = jnp.broadcast_to(locals_[r : r + 1, :], ids.shape)
         low = jnp.where(hit, jnp.minimum(low, local), low)
         high = jnp.where(hit, jnp.maximum(high, local), high)
     low = jnp.min(low, axis=1, keepdims=True)
     high = jnp.max(high, axis=1, keepdims=True)
     for r in range(rows):
-        place, local = place_ref[r : r + 1, :], local_ref[r : r + 1, :]
+        place, local = places[r : r + 1, :], locals_[r : r + 1, :]
         above = jnp.where((place == ids) & (local > low), 1, 0)
         code_ref[r : r + 1, :] = place * CAP + jnp.max(above, axis=0, keepdims=True)
     lane = lax.broadcasted_iota(jnp.int32, (devices, DH), 1)
@@ -85,7 +95,7 @@
         key_tiles = [edge_ref[:BLOCK, :], edge_ref[2 * BLOCK : 3 * BLOCK, :]]
         value_tiles = [edge_ref[BLOCK : 2 * BLOCK, :], edge_ref[3 * BLOCK :, :]]
         for i in range(FREE):
-            code = codes[step * per_step + n, i]
+            code = codes[i, step * per_step + n]
             source = code // CAP
             row = pl.multiple_of(code % CAP * BLOCK, BLOCK)
             key_tiles.append(table_ref[source, pl.ds(row, BLOCK), :])
@@ -135,23 +145,21 @@
     blocks_here = keys.shape[0] // BLOCK
     query_blocks = queries.shape[0] // QB
 
-    owner = selected // blocks_here
-    local = selected % blocks_here
-    place = owner % pb_count * kv_count + owner // pb_count
+    listed = selected.T
     first = pl.BlockSpec((BLOCK, DH), lambda i: (0, 0))
     last = pl.BlockSpec((BLOCK, DH), lambda i: (blocks_here - 1, 0))
-    held = pl.BlockSpec(selected.shape, lambda i: (0, 0))
+    held = pl.BlockSpec(listed.shape, lambda i: (0, 0))
     message_shape = (devices, 2 * PIECE, DH)
     codes, message = pl.pallas_call(
-        functools.partial(prepare, devices, blocks_here),
+        functools.partial(prepare, pb_count, kv_count, blocks_here),
         grid=(1,),
-        in_specs=[held, held, first, first, last, last],
+        in_specs=[held, first, first, last, last],
         out_specs=[held, pl.BlockSpec(message_shape, lambda i: (0, 0, 0))],
         out_shape=[
-            jax.ShapeDtypeStruct(selected.shape, jnp.int32),
+            jax.ShapeDtypeStruct(listed.shape, jnp.int32),
             jax.ShapeDtypeStruct(message_shape, jnp.bfloat16),
         ],
-    )(place, local, keys, values, keys, values)
+    )(listed, keys, values, keys, values)
 
     answer = exchange(message)
     late = (lax.axis_index(ALL) % PIECES >= PIECES // 2).astype(jnp.int32)
@@ -162,8 +170,12 @@
         functools.partial(pack, devices),
         grid_spec=pltpu.PrefetchScalarGridSpec(
             num_scalar_prefetch=1,
-            grid=(),
-            in_specs=[pl.BlockSpec(memory_space=pltpu.VMEM)] * 3,
+            grid=(1,),
+            in_specs=[
+                pl.BlockSpec(memory_space=pltpu.VMEM),
+                pl.BlockSpec(keys.shape, lambda i, c: (0, 0)),
+                pl.BlockSpec(values.shape, lambda i, c: (0, 0)),
+            ],
             out_specs=pl.BlockSpec(memory_space=pltpu.VMEM),
         ),
         out_shape=jax.ShapeDtypeStruct(parcel_shape, keys.dtype),
@@ -180,12 +192,12 @@
             grid=(query_blocks // per_step,),
             in_specs=[
                 pl.BlockSpec((per_step * QB, H * DH), lambda i, c: (i, 0)),
-                pl.BlockSpec(parcel_shape, lambda i, c: (0, 0, 0)),
+                pl.BlockSpec(memory_space=pltpu.VMEM),
             ],
             out_specs=pl.BlockSpec((per_step * QB, H * DH), lambda i, c: (i, 0)),
             scratch_shapes=[pltpu.VMEM((4 * BLOCK, DH), jnp.bfloat16)],
         ),
-        compiler_params=pltpu.CompilerParams(vmem_limit_bytes=56 << 20),
+        compiler_params=pltpu.CompilerParams(vmem_limit_bytes=(24 << 20) + parcel_bytes),
     )(codes, queries, table)
 
 

time: 96.8 us -> 92.5 us (0.956)
  Pallas kernels: 22.5 us -> 20.2 us
    pallas_call x1, Pallas kernels: 19.8 us -> 17.7 us  [per_device(): pl.pallas_call(functools.partial(attend, per_step), out_shape=jax.ShapeDt...]
    unnamed x5 -> x8, local copies, waits for them, and re-layouts: 2.86 us -> 2.09 us
where the time goes in v4:
time: 92.5 us; the launch traced here: 92.1 us
  blocking collectives  53.8 us (58%)
  Pallas kernels  20.2 us (22%)
  waiting for transfers between devices  8.39 us (9%)
  starting transfers between devices  7.3 us (8%)
  local copies, waits for them, and re-layouts  2.19 us (2%)
    all_to_all x1, blocking collectives, exchange(): return lax.all_to_all(array, ALL, split_axis=0, concat_axis=0, tiled=True)  53.8 us
    pallas_call x1, Pallas kernels, per_device(): pl.pallas_call(functools.partial(attend, per_step), out_shape=jax.ShapeDt...  17.7 us
    all_to_all x1, waiting for transfers between devices, exchange(): return lax.all_to_all(array, ALL, split_axis=0, concat_axis=0, tiled=True)  8.39 us
    all_to_all x1, starting transfers between devices, exchange(): return lax.all_to_all(array, ALL, split_axis=0, concat_axis=0, tiled=True)  7.3 us
    unnamed x8, local copies, waits for them, and re-layouts  2.09 us
  transfers between devices with their start and end apart: 1, of which 1 were waited for; matrix products, arithmetic and copies ran while one was open for 0% of the time, Pallas kernels for 0%

profile of v4, /device:TPU:0, one launch (start us, length us, event | category | flops | bytes accessed | tf_op | source)
XLA Modules:
  0.0 92.1 jit_solution(4578930386092062292)
XLA Ops:
  0.0 1.7 %shard_map.46 = (s32[14,24]{1,0:T(8,128)}, bf16[32,16,128]{2,1,0:T(8,128)(2,1)}) custom-call(s32[14,24]{1,0:T(8,128)} %bitcast.2, bf16[2048,128]{1,0:T(8,128)(2,1)} %k_ref.1, bf16[2048,128]{1,0:T(8,128)(2,1)} %v_ref.1, bf16[2048,128]{1,0:T(8,128)(2,1)} %k_ref.1, bf16[2048,128]{1,0:T(8,128)(2,1)} %v_ref.1), custom_call_target="tpu_custom_call" | custom-call | tf_op jit(solution)/shard_map/pallas_call | solution.py:153
  1.7 7.3 %all-to-all-start = ((bf16[32,16,128]{2,1,0:T(8,128)(2,1)}), bf16[32,16,128]{2,1,0:T(8,128)(2,1)S(1)}, u32[]{:S(2)}, u32[]{:S(2)}) async-start(bf16[32,16,128]{2,1,0:T(8,128)(2,1)} %get-tuple-element.8), calls=%async_computation | async-start | bytes 262144 | tf_op jit(solution)/shard_map/all_to_all | solution.py:26
  9.0 8.4 %all-to-all-done.answer_ref = bf16[32,16,128]{2,1,0:T(8,128)(2,1)S(1)} async-done(((bf16[32,16,128]{2,1,0:T(8,128)(2,1)}), bf16[32,16,128]{2,1,0:T(8,128)(2,1)S(1)}, u32[]{:S(2)}, u32[]{:S(2)}) %all-to-all-start) | async-done | bytes 131104 | tf_op jit(solution)/shard_map/all_to_all | solution.py:26
  17.4 0.1 fusion
  17.5 0.1 reshape.4
  17.6 0.1 pad_add_fusion.asked
  17.6 0.0 copy-start
  17.6 1.0 %copy-done = bf16[2048,128]{1,0:T(8,128)(2,1)S(1)} copy-done((bf16[2048,128]{1,0:T(8,128)(2,1)S(1)}, bf16[2048,128]{1,0:T(8,128)(2,1)}, u32[]{:S(2)}) %copy-start) | copy-done | bytes 524312
  18.7 0.0 copy-start.1
  18.7 1.0 %copy-done.1 = bf16[2048,128]{1,0:T(8,128)(2,1)S(1)} copy-done((bf16[2048,128]{1,0:T(8,128)(2,1)S(1)}, bf16[2048,128]{1,0:T(8,128)(2,1)}, u32[]{:S(2)}) %copy-start.1) | copy-done | bytes 524312
  19.7 0.0 copy-start.2
  19.7 0.0 copy-start.3
  19.7 0.9 shard_map.47
  20.6 53.8 %all_to_all.10.table_ref = bf16[32,264,128]{2,1,0:T(8,128)(2,1)S(1)} all-to-all(bf16[32,264,128]{2,1,0:T(8,128)(2,1)S(1)} %shard_map.47), channel_id=1, replica_groups=mesh['pb'=8,'kv'=4] {'pb','kv'}, dimensions={0} | all-to-all | bytes 4325376 | tf_op jit(solution)/shard_map/all_to_all | solution.py:26
  74.4 0.0 copy-done.2
  74.4 0.0 copy-done.3
  74.4 17.7 %shard_map.48 = bf16[1536,1024]{1,0:T(8,128)(2,1)} custom-call(s32[14,24]{1,0:T(8,128)S(1)} %copy-done.3, bf16[1536,1024]{1,0:T(8,128)(2,1)S(1)} %copy-done.2, bf16[32,264,128]{2,1,0:T(8,128)(2,1)S(1)} %all_to_all.10.table_ref), custom_call_target="tpu_custom_call" | custom-call | tf_op jit(solution)/shard_map/pallas_call | solution.py:187
Async XLA Ops:
  1.7 15.7 %all-to-all-start = ((bf16[32,16,128]{2,1,0:T(8,128)(2,1)}), bf16[32,16,128]{2,1,0:T(8,128)(2,1)S(1)}, u32[]{:S(2)}, u32[]{:S(2)}) async-start(bf16[32,16,128]{2,1,0:T(8,128)(2,1)} %get-tuple-element.8), calls=%async_computation | async-start | bytes 262144 | tf_op jit(solution)/shard_map/all_to_all | solution.py:26
  17.6 1.0 %copy-start = (bf16[2048,128]{1,0:T(8,128)(2,1)S(1)}, bf16[2048,128]{1,0:T(8,128)(2,1)}, u32[]{:S(2)}) copy-start(bf16[2048,128]{1,0:T(8,128)(2,1)} %k_ref.1) | copy-start | bytes 1572868
  18.7 1.0 %copy-start.1 = (bf16[2048,128]{1,0:T(8,128)(2,1)S(1)}, bf16[2048,128]{1,0:T(8,128)(2,1)}, u32[]{:S(2)}) copy-start(bf16[2048,128]{1,0:T(8,128)(2,1)} %v_ref.1) | copy-start | bytes 1572868
  19.7 54.7 %copy-start.2 = (bf16[1536,1024]{1,0:T(8,128)(2,1)S(1)}, bf16[1536,1024]{1,0:T(8,128)(2,1)}, u32[]{:S(2)}) copy-start(bf16[1536,1024]{1,0:T(8,128)(2,1)} %q_ref.1) | copy-start | bytes 9437188
  19.7 54.7 %copy-start.3 = (s32[14,24]{1,0:T(8,128)S(1)}, s32[14,24]{1,0:T(8,128)}, u32[]{:S(2)}) copy-start(s32[14,24]{1,0:T(8,128)} %get-tuple-element.7.codes) | copy-start | bytes 4036

commit v5 on v4

--- a/solution.py
+++ b/solution.py
@@ -62,7 +62,12 @@
         message_ref[at : at + PIECES, PIECE:, :] = edges
 
 
-def pack(devices, asked, answer_ref, k_ref, v_ref, parcel_ref):
+def stage(k_ref, v_ref, held_ref):
+    held_ref[0] = k_ref[...]
+    held_ref[1] = v_ref[...]
+
+
+def pack(devices, asked, answer_ref, held_ref, parcel_ref):
     late = asked[devices * CAP]
     piece = answer_ref[late * (devices - 1), PIECE:, :]
 
@@ -71,9 +76,9 @@
         for slot in range(CAP):
             row = pl.multiple_of(asked[m * CAP + slot] * BLOCK, BLOCK)
             at = slot * BLOCK
-            parcel_ref[m, at : at + BLOCK, :] = k_ref[pl.ds(row, BLOCK), :]
+            parcel_ref[m, at : at + BLOCK, :] = held_ref[0, pl.ds(row, BLOCK), :]
             at += CAP * BLOCK
-            parcel_ref[m, at : at + BLOCK, :] = v_ref[pl.ds(row, BLOCK), :]
+            parcel_ref[m, at : at + BLOCK, :] = held_ref[1, pl.ds(row, BLOCK), :]
         parcel_ref[m, 2 * CAP * BLOCK :, :] = piece
 
 
@@ -161,6 +166,17 @@
         ],
     )(listed, keys, values, keys, values)
 
+    held_tiles = pl.pallas_call(
+        stage,
+        grid=(1,),
+        in_specs=[
+            pl.BlockSpec(keys.shape, lambda i: (0, 0)),
+            pl.BlockSpec(values.shape, lambda i: (0, 0)),
+        ],
+        out_specs=pl.BlockSpec(memory_space=pltpu.VMEM),
+        out_shape=jax.ShapeDtypeStruct((2,) + keys.shape, keys.dtype),
+        compiler_params=pltpu.CompilerParams(vmem_limit_bytes=8 << 20),
+    )(keys, values)
     answer = exchange(message)
     late = (lax.axis_index(ALL) % PIECES >= PIECES // 2).astype(jnp.int32)
     asked = jnp.concatenate([answer[:, 0, :CAP].astype(jnp.int32).reshape(-1), late[None]])
@@ -171,19 +187,15 @@
         grid_spec=pltpu.PrefetchScalarGridSpec(
             num_scalar_prefetch=1,
             grid=(1,),
-            in_specs=[
-                pl.BlockSpec(memory_space=pltpu.VMEM),
-                pl.BlockSpec(keys.shape, lambda i, c: (0, 0)),
-                pl.BlockSpec(values.shape, lambda i, c: (0, 0)),
-            ],
+            in_specs=[pl.BlockSpec(memory_space=pltpu.VMEM)] * 2,
             out_specs=pl.BlockSpec(memory_space=pltpu.VMEM),
         ),
         out_shape=jax.ShapeDtypeStruct(parcel_shape, keys.dtype),
         compiler_params=pltpu.CompilerParams(vmem_limit_bytes=(8 << 20) + parcel_bytes),
-    )(asked, answer, keys, values)
+    )(asked, answer, held_tiles)
     table = exchange(parcel)
 
-    per_step = math.gcd(query_blocks, 6)
+    per_step = math.gcd(query_blocks, 12)
     return pl.pallas_call(
         functools.partial(attend, per_step),
         out_shape=jax.ShapeDtypeStruct(queries.shape, queries.dtype),

time: 92.5 us -> 89.8 us (0.971)
  waiting for transfers between devices: 8.39 us -> 6.22 us
    all_to_all x1, waiting for transfers between devices: 8.39 us -> 6.22 us  [exchange(): return lax.all_to_all(array, ALL, split_axis=0, concat_axis=0, tiled=True)]
where the time goes in v5:
time: 89.8 us; the launch traced here: 89.5 us
  blocking collectives  53.8 us (60%)
  Pallas kernels  19.8 us (22%)
  starting transfers between devices  7.3 us (8%)
  waiting for transfers between devices  6.22 us (7%)
  local copies, waits for them, and re-layouts  2.19 us (2%)
    all_to_all x1, blocking collectives, exchange(): return lax.all_to_all(array, ALL, split_axis=0, concat_axis=0, tiled=True)  53.8 us
    pallas_call x1, Pallas kernels, per_device(): pl.pallas_call(functools.partial(attend, per_step), out_shape=jax.ShapeDt...  17.1 us
    all_to_all x1, starting transfers between devices, exchange(): return lax.all_to_all(array, ALL, split_axis=0, concat_axis=0, tiled=True)  7.3 us
    all_to_all x1, waiting for transfers between devices, exchange(): return lax.all_to_all(array, ALL, split_axis=0, concat_axis=0, tiled=True)  6.22 us
    unnamed x8, local copies, waits for them, and re-layouts  2.09 us
  transfers between devices with their start and end apart: 1, of which 1 were waited for; matrix products, arithmetic and copies ran while one was open for 0% of the time, Pallas kernels for 0%

profile of v5, /device:TPU:0, one launch (start us, length us, event | category | flops | bytes accessed | tf_op | source)
XLA Modules:
  0.0 89.5 jit_solution(12127064191888989002)
XLA Ops:
  0.0 1.7 %shard_map.46 = (s32[14,24]{1,0:T(8,128)}, bf16[32,16,128]{2,1,0:T(8,128)(2,1)}) custom-call(s32[14,24]{1,0:T(8,128)} %bitcast.2, bf16[2048,128]{1,0:T(8,128)(2,1)} %k_ref.1, bf16[2048,128]{1,0:T(8,128)(2,1)} %v_ref.1, bf16[2048,128]{1,0:T(8,128)(2,1)} %k_ref.1, bf16[2048,128]{1,0:T(8,128)(2,1)} %v_ref.1), custom_call_target="tpu_custom_call" | custom-call | tf_op jit(solution)/shard_map/pallas_call | solution.py:158
  1.7 7.3 %all-to-all-start = ((bf16[32,16,128]{2,1,0:T(8,128)(2,1)}), bf16[32,16,128]{2,1,0:T(8,128)(2,1)S(1)}, u32[]{:S(2)}, u32[]{:S(2)}) async-start(bf16[32,16,128]{2,1,0:T(8,128)(2,1)} %get-tuple-element.8), calls=%async_computation | async-start | bytes 262144 | tf_op jit(solution)/shard_map/all_to_all | solution.py:26
  9.0 0.0 copy-start
  9.0 1.0 %copy-done = bf16[2048,128]{1,0:T(8,128)(2,1)S(1)} copy-done((bf16[2048,128]{1,0:T(8,128)(2,1)S(1)}, bf16[2048,128]{1,0:T(8,128)(2,1)}, u32[]{:S(2)}) %copy-start) | copy-done | bytes 524312
  10.1 0.0 copy-start.1
  10.1 1.0 %copy-done.1 = bf16[2048,128]{1,0:T(8,128)(2,1)S(1)} copy-done((bf16[2048,128]{1,0:T(8,128)(2,1)S(1)}, bf16[2048,128]{1,0:T(8,128)(2,1)}, u32[]{:S(2)}) %copy-start.1) | copy-done | bytes 524312
  11.1 0.1 shard_map.47.held_ref
  11.2 6.2 %all-to-all-done.answer_ref = bf16[32,16,128]{2,1,0:T(8,128)(2,1)S(1)} async-done(((bf16[32,16,128]{2,1,0:T(8,128)(2,1)}), bf16[32,16,128]{2,1,0:T(8,128)(2,1)S(1)}, u32[]{:S(2)}, u32[]{:S(2)}) %all-to-all-start) | async-done | bytes 131104 | tf_op jit(solution)/shard_map/all_to_all | solution.py:26
  17.4 0.1 fusion
  17.5 0.1 reshape.4
  17.6 0.1 pad_add_fusion.asked
  17.6 0.0 copy-start.2
  17.6 0.0 copy-start.3
  17.7 0.9 shard_map.48
  18.5 53.8 %all_to_all.10.table_ref = bf16[32,264,128]{2,1,0:T(8,128)(2,1)S(1)} all-to-all(bf16[32,264,128]{2,1,0:T(8,128)(2,1)S(1)} %shard_map.48), channel_id=1, replica_groups=mesh['pb'=8,'kv'=4] {'pb','kv'}, dimensions={0} | all-to-all | bytes 4325376 | tf_op jit(solution)/shard_map/all_to_all | solution.py:26
  72.3 0.0 copy-done.2
  72.3 0.0 copy-done.3
  72.4 17.1 %shard_map.49 = bf16[1536,1024]{1,0:T(8,128)(2,1)} custom-call(s32[14,24]{1,0:T(8,128)S(1)} %copy-done.3, bf16[1536,1024]{1,0:T(8,128)(2,1)S(1)} %copy-done.2, bf16[32,264,128]{2,1,0:T(8,128)(2,1)S(1)} %all_to_all.10.table_ref), custom_call_target="tpu_custom_call" | custom-call | tf_op jit(solution)/shard_map/pallas_call | solution.py:199
Async XLA Ops:
  1.7 15.7 %all-to-all-start = ((bf16[32,16,128]{2,1,0:T(8,128)(2,1)}), bf16[32,16,128]{2,1,0:T(8,128)(2,1)S(1)}, u32[]{:S(2)}, u32[]{:S(2)}) async-start(bf16[32,16,128]{2,1,0:T(8,128)(2,1)} %get-tuple-element.8), calls=%async_computation | async-start | bytes 262144 | tf_op jit(solution)/shard_map/all_to_all | solution.py:26
  9.0 1.0 %copy-start = (bf16[2048,128]{1,0:T(8,128)(2,1)S(1)}, bf16[2048,128]{1,0:T(8,128)(2,1)}, u32[]{:S(2)}) copy-start(bf16[2048,128]{1,0:T(8,128)(2,1)} %k_ref.1) | copy-start | bytes 1572868
  10.1 1.0 %copy-start.1 = (bf16[2048,128]{1,0:T(8,128)(2,1)S(1)}, bf16[2048,128]{1,0:T(8,128)(2,1)}, u32[]{:S(2)}) copy-start(bf16[2048,128]{1,0:T(8,128)(2,1)} %v_ref.1) | copy-start | bytes 1572868
  17.6 54.7 %copy-start.2 = (bf16[1536,1024]{1,0:T(8,128)(2,1)S(1)}, bf16[1536,1024]{1,0:T(8,128)(2,1)}, u32[]{:S(2)}) copy-start(bf16[1536,1024]{1,0:T(8,128)(2,1)} %q_ref.1) | copy-start | bytes 9437188
  17.6 54.7 %copy-start.3 = (s32[14,24]{1,0:T(8,128)S(1)}, s32[14,24]{1,0:T(8,128)}, u32[]{:S(2)}) copy-start(s32[14,24]{1,0:T(8,128)} %get-tuple-element.7.codes) | copy-start | bytes 4036

commit v6 on v5

--- a/solution.py
+++ b/solution.py
@@ -18,6 +18,7 @@
 PIECE = 4 * BLOCK // PIECES
 CHUNK = 256
 GROUP = 4
+TRUSTED = 2.0 ** 100
 SCALE = DH ** -0.5 * math.log2(math.e)
 ALL = ("pb", "kv")
 
@@ -67,9 +68,8 @@
     held_ref[1] = v_ref[...]
 
 
-def pack(devices, asked, answer_ref, held_ref, parcel_ref):
-    late = asked[devices * CAP]
-    piece = answer_ref[late * (devices - 1), PIECE:, :]
+def pack(devices, asked, late, answer_ref, held_ref, parcel_ref):
+    piece = answer_ref[late[0] * (devices - 1), PIECE:, :]
 
     @pl.loop(0, devices)
     def _(m):
@@ -95,7 +95,7 @@
     chunks = QB * H // CHUNK
 
     def load(n):
-        rows = q_ref[n * QB : (n + 1) * QB, :]
+        rows = q_ref[pl.ds(pl.multiple_of(n * QB, QB), QB), :]
         stacked = jnp.concatenate([rows[:, h * DH : (h + 1) * DH] for h in range(H)], axis=0)
         key_tiles = [edge_ref[:BLOCK, :], edge_ref[2 * BLOCK : 3 * BLOCK, :]]
         value_tiles = [edge_ref[BLOCK : 2 * BLOCK, :], edge_ref[3 * BLOCK :, :]]
@@ -112,35 +112,59 @@
             [jnp.concatenate([join(value_tiles, g), ones], axis=1) for g in range(groups)],
         )
 
-    def score(block, c):
+    def score(block, c, g):
         part = block[0][c * CHUNK : (c + 1) * CHUNK]
-        scores = [
-            lax.dot_general(part, k, (((1,), (1,)), ((), ())), preferred_element_type=jnp.float32)
-            for k in block[1]
-        ]
-        tops = [jnp.max(s, axis=1, keepdims=True) for s in scores]
-        return scores, functools.reduce(jnp.maximum, tops)
-
-    def finish(block, n, c, scores, top):
-        total = None
-        for s, v in zip(scores, block[2]):
-            weights = jnp.exp2((s - top) * SCALE).astype(jnp.bfloat16)
-            product = jnp.dot(weights, v, preferred_element_type=jnp.float32)
-            total = product if total is None else total + product
+        return lax.dot_general(
+            part, block[1][g], (((1,), (1,)), ((), ())), preferred_element_type=jnp.float32
+        )
+
+    def weigh(block, g, scores, shift):
+        weights = jnp.exp2((scores - shift) * SCALE).astype(jnp.bfloat16)
+        return jnp.dot(weights, block[2][g], preferred_element_type=jnp.float32)
+
+    def store(n, c, total):
         done = (total[:, :DH] / total[:, DH:]).astype(jnp.bfloat16)
         for i in range(CHUNK // QB):
             h = c * (CHUNK // QB) + i
-            out_ref[n * QB : (n + 1) * QB, h * DH : (h + 1) * DH] = done[i * QB : (i + 1) * QB]
-
-    waiting = None
+            row = pl.multiple_of(n * QB, QB)
+            out_ref[pl.ds(row, QB), h * DH : (h + 1) * DH] = done[i * QB : (i + 1) * QB]
+
+    largest, total, waiting = None, None, None
+
+    def advance(block, n, c, g, scores, shift):
+        nonlocal largest, total
+        product = weigh(block, g, scores, shift)
+        total = product if g == 0 else total + product
+        if g == groups - 1:
+            sums = total[:, DH:]
+            parts = [sums[i * 8 : (i + 1) * 8] for i in range(CHUNK // 8)]
+            largest = functools.reduce(jnp.maximum, parts if largest is None else [largest, *parts])
+            store(n, c, total)
+
     for n in range(per_step):
         block = load(n)
         for c in range(chunks):
-            scored = (block, n, c, *score(block, c))
-            if waiting is not None:
-                finish(*waiting)
-            waiting = scored
-    finish(*waiting)
+            shift = None
+            for g in range(groups):
+                scores = score(block, c, g)
+                if g == 0:
+                    shift = jnp.max(scores, axis=1, keepdims=True)
+                if waiting is not None:
+                    advance(*waiting)
+                waiting = (block, n, c, g, scores, shift)
+    advance(*waiting)
+
+    @pl.when(jnp.logical_not(jnp.max(largest) < TRUSTED))
+    def _():
+        @pl.loop(0, per_step)
+        def _(n):
+            block = load(n)
+            for c in range(chunks):
+                scores = [score(block, c, g) for g in range(groups)]
+                tops = [jnp.max(s, axis=1, keepdims=True) for s in scores]
+                top = functools.reduce(jnp.maximum, tops)
+                products = [weigh(block, g, scores[g], top) for g in range(groups)]
+                store(n, c, functools.reduce(jnp.add, products))
 
 
 def per_device(queries, keys, values, selected):
@@ -179,20 +203,20 @@
     )(keys, values)
     answer = exchange(message)
     late = (lax.axis_index(ALL) % PIECES >= PIECES // 2).astype(jnp.int32)
-    asked = jnp.concatenate([answer[:, 0, :CAP].astype(jnp.int32).reshape(-1), late[None]])
+    asked = answer[:, 0, :CAP].astype(jnp.int32).reshape(-1)
     parcel_shape = (devices, 2 * CAP * BLOCK + PIECE, DH)
     parcel_bytes = 2 * math.prod(parcel_shape)
     parcel = pl.pallas_call(
         functools.partial(pack, devices),
         grid_spec=pltpu.PrefetchScalarGridSpec(
-            num_scalar_prefetch=1,
+            num_scalar_prefetch=2,
             grid=(1,),
             in_specs=[pl.BlockSpec(memory_space=pltpu.VMEM)] * 2,
             out_specs=pl.BlockSpec(memory_space=pltpu.VMEM),
         ),
         out_shape=jax.ShapeDtypeStruct(parcel_shape, keys.dtype),
         compiler_params=pltpu.CompilerParams(vmem_limit_bytes=(8 << 20) + parcel_bytes),
-    )(asked, answer, held_tiles)
+    )(asked, late[None], answer, held_tiles)
     table = exchange(parcel)
 
     per_step = math.gcd(query_blocks, 12)

time: 89.8 us -> 89.1 us (level)
  no operation moved by 1% of the time
where the time goes in v6:
time: 89.1 us; the launch traced here: 88.7 us
  blocking collectives  53.8 us (60%)
  Pallas kernels  19.1 us (21%)
  starting transfers between devices  7.3 us (8%)
  waiting for transfers between devices  6.22 us (7%)
  local copies, waits for them, and re-layouts  2.19 us (2%)
    all_to_all x1, blocking collectives, exchange(): return lax.all_to_all(array, ALL, split_axis=0, concat_axis=0, tiled=True)  53.8 us
    pallas_call x1, Pallas kernels, per_device(): pl.pallas_call(functools.partial(attend, per_step), out_shape=jax.ShapeDt...  16.4 us
    all_to_all x1, starting transfers between devices, exchange(): return lax.all_to_all(array, ALL, split_axis=0, concat_axis=0, tiled=True)  7.3 us
    all_to_all x1, waiting for transfers between devices, exchange(): return lax.all_to_all(array, ALL, split_axis=0, concat_axis=0, tiled=True)  6.22 us
    unnamed x8, local copies, waits for them, and re-layouts  2.09 us
  transfers between devices with their start and end apart: 1, of which 1 were waited for; matrix products, arithmetic and copies ran while one was open for 0% of the time, Pallas kernels for 0%

profile of v6, /device:TPU:0, one launch (start us, length us, event | category | flops | bytes accessed | tf_op | source)
XLA Modules:
  0.0 88.7 jit_solution(18113589671058750098)
XLA Ops:
  0.0 1.7 %shard_map.46 = (s32[14,24]{1,0:T(8,128)}, bf16[32,16,128]{2,1,0:T(8,128)(2,1)}) custom-call(s32[14,24]{1,0:T(8,128)} %bitcast.2, bf16[2048,128]{1,0:T(8,128)(2,1)} %k_ref.1, bf16[2048,128]{1,0:T(8,128)(2,1)} %v_ref.1, bf16[2048,128]{1,0:T(8,128)(2,1)} %k_ref.1, bf16[2048,128]{1,0:T(8,128)(2,1)} %v_ref.1), custom_call_target="tpu_custom_call" | custom-call | tf_op jit(solution)/shard_map/pallas_call | solution.py:182
  1.7 7.3 %all-to-all-start = ((bf16[32,16,128]{2,1,0:T(8,128)(2,1)}), bf16[32,16,128]{2,1,0:T(8,128)(2,1)S(1)}, u32[]{:S(2)}, u32[]{:S(2)}) async-start(bf16[32,16,128]{2,1,0:T(8,128)(2,1)} %get-tuple-element.8), calls=%async_computation | async-start | bytes 262144 | tf_op jit(solution)/shard_map/all_to_all | solution.py:27
  9.0 0.0 copy-start
  9.0 1.0 %copy-done = bf16[2048,128]{1,0:T(8,128)(2,1)S(1)} copy-done((bf16[2048,128]{1,0:T(8,128)(2,1)S(1)}, bf16[2048,128]{1,0:T(8,128)(2,1)}, u32[]{:S(2)}) %copy-start) | copy-done | bytes 524312
  10.1 0.0 copy-start.1
  10.1 1.0 %copy-done.1 = bf16[2048,128]{1,0:T(8,128)(2,1)S(1)} copy-done((bf16[2048,128]{1,0:T(8,128)(2,1)S(1)}, bf16[2048,128]{1,0:T(8,128)(2,1)}, u32[]{:S(2)}) %copy-start.1) | copy-done | bytes 524312
  11.1 0.1 shard_map.47.held_ref
  11.2 6.2 %all-to-all-done.answer_ref = bf16[32,16,128]{2,1,0:T(8,128)(2,1)S(1)} async-done(((bf16[32,16,128]{2,1,0:T(8,128)(2,1)}), bf16[32,16,128]{2,1,0:T(8,128)(2,1)S(1)}, u32[]{:S(2)}, u32[]{:S(2)}) %all-to-all-start) | async-done | bytes 131104 | tf_op jit(solution)/shard_map/all_to_all | solution.py:27
  17.4 0.1 fusion
  17.5 0.1 reshape.4.asked
  17.6 0.0 copy-start.2
  17.6 0.0 copy-start.3
  17.6 0.9 shard_map.48
  18.5 53.8 %all_to_all.10.table_ref = bf16[32,264,128]{2,1,0:T(8,128)(2,1)S(1)} all-to-all(bf16[32,264,128]{2,1,0:T(8,128)(2,1)S(1)} %shard_map.48), channel_id=1, replica_groups=mesh['pb'=8,'kv'=4] {'pb','kv'}, dimensions={0} | all-to-all | bytes 4325376 | tf_op jit(solution)/shard_map/all_to_all | solution.py:27
  72.3 0.0 copy-done.2
  72.3 0.0 copy-done.3
  72.3 16.4 %shard_map.49 = bf16[1536,1024]{1,0:T(8,128)(2,1)} custom-call(s32[14,24]{1,0:T(8,128)S(1)} %copy-done.3, bf16[1536,1024]{1,0:T(8,128)(2,1)S(1)} %copy-done.2, bf16[32,264,128]{2,1,0:T(8,128)(2,1)S(1)} %all_to_all.10.table_ref), custom_call_target="tpu_custom_call" | custom-call | tf_op jit(solution)/shard_map/pallas_call | solution.py:223
Async XLA Ops:
  1.7 15.7 %all-to-all-start = ((bf16[32,16,128]{2,1,0:T(8,128)(2,1)}), bf16[32,16,128]{2,1,0:T(8,128)(2,1)S(1)}, u32[]{:S(2)}, u32[]{:S(2)}) async-start(bf16[32,16,128]{2,1,0:T(8,128)(2,1)} %get-tuple-element.8), calls=%async_computation | async-start | bytes 262144 | tf_op jit(solution)/shard_map/all_to_all | solution.py:27
  9.0 1.0 %copy-start = (bf16[2048,128]{1,0:T(8,128)(2,1)S(1)}, bf16[2048,128]{1,0:T(8,128)(2,1)}, u32[]{:S(2)}) copy-start(bf16[2048,128]{1,0:T(8,128)(2,1)} %k_ref.1) | copy-start | bytes 1572868
  10.1 1.0 %copy-start.1 = (bf16[2048,128]{1,0:T(8,128)(2,1)S(1)}, bf16[2048,128]{1,0:T(8,128)(2,1)}, u32[]{:S(2)}) copy-start(bf16[2048,128]{1,0:T(8,128)(2,1)} %v_ref.1) | copy-start | bytes 1572868
  17.6 54.7 %copy-start.2 = (bf16[1536,1024]{1,0:T(8,128)(2,1)S(1)}, bf16[1536,1024]{1,0:T(8,128)(2,1)}, u32[]{:S(2)}) copy-start(bf16[1536,1024]{1,0:T(8,128)(2,1)} %q_ref.1) | copy-start | bytes 9437188
  17.6 54.7 %copy-start.3 = (s32[14,24]{1,0:T(8,128)S(1)}, s32[14,24]{1,0:T(8,128)}, u32[]{:S(2)}) copy-start(s32[14,24]{1,0:T(8,128)} %get-tuple-element.7.codes) | copy-start | bytes 4036

commit v7 on v6

--- a/solution.py
+++ b/solution.py
@@ -15,7 +15,8 @@
 QB = 64
 CAP = 2
 PIECES = 32
-PIECE = 4 * BLOCK // PIECES
+PIECE = 2 * BLOCK // PIECES
+TILE = 2 * PIECE
 CHUNK = 256
 GROUP = 4
 TRUSTED = 2.0 ** 100
@@ -33,7 +34,11 @@
     return array // n, array % n
 
 
-def prepare(pb_count, kv_count, blocks_here, selected_ref, fk, fv, lk, lv, code_ref, message_ref):
+def roll_half(tile):
+    return jnp.concatenate([tile[PIECE:], tile[:PIECE]], axis=0)
+
+
+def prepare(pb_count, kv_count, blocks_here, me_ref, selected_ref, fk, fv, lk, lv, code_ref, message_ref):
     devices = pb_count * kv_count
     rows, columns = selected_ref.shape
     owner, locals_ = divide(selected_ref[...], blocks_here)
@@ -55,12 +60,15 @@
         code_ref[r : r + 1, :] = place * CAP + jnp.max(above, axis=0, keepdims=True)
     lane = lax.broadcasted_iota(jnp.int32, (devices, DH), 1)
     wants = jnp.where(lane == 0, low, jnp.where(lane == 1, high, 0)).astype(jnp.float32)
-    wants = jnp.broadcast_to(wants[:, None, :], (devices, PIECE, DH))
-    message_ref[:, :PIECE, :] = wants.astype(jnp.bfloat16)
-    edges = jnp.concatenate([fk[...], fv[...], lk[...], lv[...]], axis=0).astype(jnp.float32)
-    edges = edges.reshape(PIECES, PIECE, DH).astype(jnp.bfloat16)
-    for at in range(0, devices, PIECES):
-        message_ref[at : at + PIECES, PIECE:, :] = edges
+    first = me_ref[0] == 0
+    edge = jnp.concatenate([jnp.where(first, fk[...], lk[...]), jnp.where(first, fv[...], lv[...])], axis=0)
+    edge = edge.astype(jnp.float32)
+    upper = lax.broadcasted_iota(jnp.int32, (TILE, DH), 0) < PIECE
+    for m in range(devices):
+        at = m % PIECES // 2 * TILE
+        piece = edge[at : at + TILE]
+        piece = piece if m % 2 == 0 else roll_half(piece)
+        message_ref[m] = jnp.where(upper, piece, wants[m : m + 1]).astype(jnp.bfloat16)
 
 
 def stage(k_ref, v_ref, held_ref):
@@ -68,10 +76,12 @@
     held_ref[1] = v_ref[...]
 
 
-def pack(devices, asked, late, answer_ref, held_ref, parcel_ref):
-    piece = answer_ref[late[0] * (devices - 1), PIECE:, :]
-
-    @pl.loop(0, devices)
+def pack(devices, asked, answer_ref, held_ref, parcel_ref):
+    first = answer_ref[0].astype(jnp.float32)
+    last = answer_ref[devices - 1].astype(jnp.float32)
+    piece = jnp.concatenate([first[:PIECE], last[:PIECE]], axis=0).astype(jnp.bfloat16)
+
+    @pl.loop(0, devices, unroll=4)
     def _(m):
         for slot in range(CAP):
             row = pl.multiple_of(asked[m * CAP + slot] * BLOCK, BLOCK)
@@ -87,8 +97,14 @@
 
     @pl.when(step == 0)
     def _():
-        edges = table_ref[:PIECES, 2 * CAP * BLOCK :, :].astype(jnp.float32)
-        edge_ref[...] = edges.reshape(4 * BLOCK, DH).astype(jnp.bfloat16)
+        upper = lax.broadcasted_iota(jnp.int32, (TILE, DH), 0) < PIECE
+        firsts, lasts = [], []
+        for p in range(0, PIECES, 2):
+            even = table_ref[p, 2 * CAP * BLOCK :, :].astype(jnp.float32)
+            odd = table_ref[p + 1, 2 * CAP * BLOCK :, :].astype(jnp.float32)
+            firsts.append(jnp.where(upper, even, roll_half(odd)))
+            lasts.append(jnp.where(upper, roll_half(even), odd))
+        edge_ref[...] = jnp.concatenate(firsts + lasts, axis=0).astype(jnp.bfloat16)
 
     ones = jnp.ones((GROUP * BLOCK, DH), jnp.bfloat16)
     groups = (FREE + 2) // GROUP
@@ -175,20 +191,24 @@
     query_blocks = queries.shape[0] // QB
 
     listed = selected.T
-    first = pl.BlockSpec((BLOCK, DH), lambda i: (0, 0))
-    last = pl.BlockSpec((BLOCK, DH), lambda i: (blocks_here - 1, 0))
-    held = pl.BlockSpec(listed.shape, lambda i: (0, 0))
-    message_shape = (devices, 2 * PIECE, DH)
+    me = lax.axis_index(ALL).astype(jnp.int32)[None]
+    first = pl.BlockSpec((BLOCK, DH), lambda i, m: (0, 0))
+    last = pl.BlockSpec((BLOCK, DH), lambda i, m: (blocks_here - 1, 0))
+    held = pl.BlockSpec(listed.shape, lambda i, m: (0, 0))
+    message_shape = (devices, TILE, DH)
     codes, message = pl.pallas_call(
         functools.partial(prepare, pb_count, kv_count, blocks_here),
-        grid=(1,),
-        in_specs=[held, first, first, last, last],
-        out_specs=[held, pl.BlockSpec(message_shape, lambda i: (0, 0, 0))],
+        grid_spec=pltpu.PrefetchScalarGridSpec(
+            num_scalar_prefetch=1,
+            grid=(1,),
+            in_specs=[held, first, first, last, last],
+            out_specs=[held, pl.BlockSpec(message_shape, lambda i, m: (0, 0, 0))],
+        ),
         out_shape=[
             jax.ShapeDtypeStruct(listed.shape, jnp.int32),
             jax.ShapeDtypeStruct(message_shape, jnp.bfloat16),
         ],
-    )(listed, keys, values, keys, values)
+    )(me, listed, keys, values, keys, values)
 
     held_tiles = pl.pallas_call(
         stage,
@@ -202,21 +222,20 @@
         compiler_params=pltpu.CompilerParams(vmem_limit_bytes=8 << 20),
     )(keys, values)
     answer = exchange(message)
-    late = (lax.axis_index(ALL) % PIECES >= PIECES // 2).astype(jnp.int32)
-    asked = answer[:, 0, :CAP].astype(jnp.int32).reshape(-1)
-    parcel_shape = (devices, 2 * CAP * BLOCK + PIECE, DH)
+    asked = answer[:, PIECE, :CAP].astype(jnp.int32).reshape(-1)
+    parcel_shape = (devices, 2 * CAP * BLOCK + TILE, DH)
     parcel_bytes = 2 * math.prod(parcel_shape)
     parcel = pl.pallas_call(
         functools.partial(pack, devices),
         grid_spec=pltpu.PrefetchScalarGridSpec(
-            num_scalar_prefetch=2,
+            num_scalar_prefetch=1,
             grid=(1,),
             in_specs=[pl.BlockSpec(memory_space=pltpu.VMEM)] * 2,
             out_specs=pl.BlockSpec(memory_space=pltpu.VMEM),
         ),
         out_shape=jax.ShapeDtypeStruct(parcel_shape, keys.dtype),
         compiler_params=pltpu.CompilerParams(vmem_limit_bytes=(8 << 20) + parcel_bytes),
-    )(asked, late[None], answer, held_tiles)
+    )(asked, answer, held_tiles)
     table = exchange(parcel)
 
     per_step = math.gcd(query_blocks, 12)

time: 89.1 us -> 88 us (0.988)
  no operation moved by 1% of the time
where the time goes in v7:
time: 88 us; the launch traced here: 87.6 us
  blocking collectives  53.8 us (61%)
  Pallas kernels  18.9 us (21%)
  starting transfers between devices  7.3 us (8%)
  waiting for transfers between devices  5.34 us (6%)
  local copies, waits for them, and re-layouts  2.19 us (2%)
    all_to_all x1, blocking collectives, exchange(): return lax.all_to_all(array, ALL, split_axis=0, concat_axis=0, tiled=True)  53.8 us
    pallas_call x1, Pallas kernels, per_device(): pl.pallas_call(functools.partial(attend, per_step), out_shape=jax.ShapeDt...  16.4 us
    all_to_all x1, starting transfers between devices, exchange(): return lax.all_to_all(array, ALL, split_axis=0, concat_axis=0, tiled=True)  7.3 us
    all_to_all x1, waiting for transfers between devices, exchange(): return lax.all_to_all(array, ALL, split_axis=0, concat_axis=0, tiled=True)  5.34 us
    unnamed x8, local copies, waits for them, and re-layouts  2.09 us
  transfers between devices with their start and end apart: 1, of which 1 were waited for; matrix products, arithmetic and copies ran while one was open for 0% of the time, Pallas kernels for 0%

profile of v7, /device:TPU:0, one launch (start us, length us, event | category | flops | bytes accessed | tf_op | source)
XLA Modules:
  0.0 87.6 jit_solution(15180316061691298413)
XLA Ops:
  0.0 1.7 %shard_map.46 = (s32[14,24]{1,0:T(8,128)}, bf16[32,8,128]{2,1,0:T(8,128)(2,1)}) custom-call(s32[1]{0:T(128)} %bitcast.me_ref, s32[14,24]{1,0:T(8,128)} %bitcast.2, bf16[2048,128]{1,0:T(8,128)(2,1)} %k_ref.1, bf16[2048,128]{1,0:T(8,128)(2,1)} %v_ref.1, bf16[2048,128]{1,0:T(8,128)(2,1)} %k_ref.1, bf16[2048,128]{1,0:T(8,128)(2,1)} %v_ref.1), custom_call_target="tpu_custom_call" | custom-call | tf_op jit(solution)/shard_map/pallas_call | solution.py:199
  1.7 7.3 %all-to-all-start = ((bf16[32,8,128]{2,1,0:T(8,128)(2,1)}), bf16[32,8,128]{2,1,0:T(8,128)(2,1)S(1)}, u32[]{:S(2)}, u32[]{:S(2)}) async-start(bf16[32,8,128]{2,1,0:T(8,128)(2,1)} %get-tuple-element.8), calls=%async_computation | async-start | bytes 131072 | tf_op jit(solution)/shard_map/all_to_all | solution.py:28
  9.0 0.0 copy-start
  9.0 1.0 %copy-done = bf16[2048,128]{1,0:T(8,128)(2,1)S(1)} copy-done((bf16[2048,128]{1,0:T(8,128)(2,1)S(1)}, bf16[2048,128]{1,0:T(8,128)(2,1)}, u32[]{:S(2)}) %copy-start) | copy-done | bytes 524312
  10.0 0.0 copy-start.1
  10.0 1.0 %copy-done.1 = bf16[2048,128]{1,0:T(8,128)(2,1)S(1)} copy-done((bf16[2048,128]{1,0:T(8,128)(2,1)S(1)}, bf16[2048,128]{1,0:T(8,128)(2,1)}, u32[]{:S(2)}) %copy-start.1) | copy-done | bytes 524312
  11.1 0.1 shard_map.47.held_ref
  11.1 5.3 %all-to-all-done.answer_ref = bf16[32,8,128]{2,1,0:T(8,128)(2,1)S(1)} async-done(((bf16[32,8,128]{2,1,0:T(8,128)(2,1)}), bf16[32,8,128]{2,1,0:T(8,128)(2,1)S(1)}, u32[]{:S(2)}, u32[]{:S(2)}) %all-to-all-start) | async-done | bytes 65568 | tf_op jit(solution)/shard_map/all_to_all | solution.py:28
  16.5 0.1 fusion
  16.5 0.1 reshape.4.asked
  16.6 0.0 copy-start.2
  16.7 0.0 copy-start.3
  16.7 0.7 shard_map.48
  17.4 53.8 %all_to_all.10.table_ref = bf16[32,264,128]{2,1,0:T(8,128)(2,1)S(1)} all-to-all(bf16[32,264,128]{2,1,0:T(8,128)(2,1)S(1)} %shard_map.48), channel_id=1, replica_groups=mesh['pb'=8,'kv'=4] {'pb','kv'}, dimensions={0} | all-to-all | bytes 4325376 | tf_op jit(solution)/shard_map/all_to_all | solution.py:28
  71.2 0.0 copy-done.2
  71.2 0.0 copy-done.3
  71.2 16.4 %shard_map.49 = bf16[1536,1024]{1,0:T(8,128)(2,1)} custom-call(s32[14,24]{1,0:T(8,128)S(1)} %copy-done.3, bf16[1536,1024]{1,0:T(8,128)(2,1)S(1)} %copy-done.2, bf16[32,264,128]{2,1,0:T(8,128)(2,1)S(1)} %all_to_all.10.table_ref), custom_call_target="tpu_custom_call" | custom-call | tf_op jit(solution)/shard_map/pallas_call | solution.py:242
Async XLA Ops:
  1.7 14.8 %all-to-all-start = ((bf16[32,8,128]{2,1,0:T(8,128)(2,1)}), bf16[32,8,128]{2,1,0:T(8,128)(2,1)S(1)}, u32[]{:S(2)}, u32[]{:S(2)}) async-start(bf16[32,8,128]{2,1,0:T(8,128)(2,1)} %get-tuple-element.8), calls=%async_computation | async-start | bytes 131072 | tf_op jit(solution)/shard_map/all_to_all | solution.py:28
  9.0 1.0 %copy-start = (bf16[2048,128]{1,0:T(8,128)(2,1)S(1)}, bf16[2048,128]{1,0:T(8,128)(2,1)}, u32[]{:S(2)}) copy-start(bf16[2048,128]{1,0:T(8,128)(2,1)} %k_ref.1) | copy-start | bytes 1572868
  10.0 1.0 %copy-start.1 = (bf16[2048,128]{1,0:T(8,128)(2,1)S(1)}, bf16[2048,128]{1,0:T(8,128)(2,1)}, u32[]{:S(2)}) copy-start(bf16[2048,128]{1,0:T(8,128)(2,1)} %v_ref.1) | copy-start | bytes 1572868
  16.6 54.6 %copy-start.2 = (bf16[1536,1024]{1,0:T(8,128)(2,1)S(1)}, bf16[1536,1024]{1,0:T(8,128)(2,1)}, u32[]{:S(2)}) copy-start(bf16[1536,1024]{1,0:T(8,128)(2,1)} %q_ref.1) | copy-start | bytes 9437188
  16.7 54.6 %copy-start.3 = (s32[14,24]{1,0:T(8,128)S(1)}, s32[14,24]{1,0:T(8,128)}, u32[]{:S(2)}) copy-start(s32[14,24]{1,0:T(8,128)} %get-tuple-element.7.codes) | copy-start | bytes 4036

commit v8 on v7

--- a/solution.py
+++ b/solution.py
@@ -38,26 +38,28 @@
     return jnp.concatenate([tile[PIECE:], tile[:PIECE]], axis=0)
 
 
-def prepare(pb_count, kv_count, blocks_here, me_ref, selected_ref, fk, fv, lk, lv, code_ref, message_ref):
+def wanted(pb_count, kv_count, blocks_here, selected_ref):
     devices = pb_count * kv_count
     rows, columns = selected_ref.shape
-    owner, locals_ = divide(selected_ref[...], blocks_here)
+    owner, local = divide(selected_ref[...], blocks_here)
     owner_kv, owner_pb = divide(owner, pb_count)
-    places = owner_pb * kv_count + owner_kv
+    place = owner_pb * kv_count + owner_kv
     ids = lax.broadcasted_iota(jnp.int32, (devices, columns), 0)
     low = jnp.full((devices, columns), blocks_here - 1, jnp.int32)
     high = jnp.zeros((devices, columns), jnp.int32)
     for r in range(rows):
-        hit = places[r : r + 1, :] == ids
-        local = jnp.broadcast_to(locals_[r : r + 1, :], ids.shape)
-        low = jnp.where(hit, jnp.minimum(low, local), low)
-        high = jnp.where(hit, jnp.maximum(high, local), high)
+        hit = place[r : r + 1, :] == ids
+        here = jnp.broadcast_to(local[r : r + 1, :], ids.shape)
+        low = jnp.where(hit, jnp.minimum(low, here), low)
+        high = jnp.where(hit, jnp.maximum(high, here), high)
     low = jnp.min(low, axis=1, keepdims=True)
     high = jnp.max(high, axis=1, keepdims=True)
-    for r in range(rows):
-        place, local = places[r : r + 1, :], locals_[r : r + 1, :]
-        above = jnp.where((place == ids) & (local > low), 1, 0)
-        code_ref[r : r + 1, :] = place * CAP + jnp.max(above, axis=0, keepdims=True)
+    return place, local, ids, low, high
+
+
+def prepare(pb_count, kv_count, blocks_here, me_ref, selected_ref, fk, fv, lk, lv, message_ref):
+    devices = pb_count * kv_count
+    low, high = wanted(pb_count, kv_count, blocks_here, selected_ref)[3:]
     lane = lax.broadcasted_iota(jnp.int32, (devices, DH), 1)
     wants = jnp.where(lane == 0, low, jnp.where(lane == 1, high, 0)).astype(jnp.float32)
     first = me_ref[0] == 0
@@ -71,9 +73,14 @@
         message_ref[m] = jnp.where(upper, piece, wants[m : m + 1]).astype(jnp.bfloat16)
 
 
-def stage(k_ref, v_ref, held_ref):
+def stage(pb_count, kv_count, blocks_here, selected_ref, k_ref, v_ref, held_ref, code_ref):
     held_ref[0] = k_ref[...]
     held_ref[1] = v_ref[...]
+    places, locals_, ids, low, _ = wanted(pb_count, kv_count, blocks_here, selected_ref)
+    for r in range(selected_ref.shape[0]):
+        place, local = places[r : r + 1, :], locals_[r : r + 1, :]
+        above = jnp.where((place == ids) & (local > low), 1, 0)
+        code_ref[r : r + 1, :] = place * CAP + jnp.max(above, axis=0, keepdims=True)
 
 
 def pack(devices, asked, answer_ref, held_ref, parcel_ref):
@@ -196,31 +203,33 @@
     last = pl.BlockSpec((BLOCK, DH), lambda i, m: (blocks_here - 1, 0))
     held = pl.BlockSpec(listed.shape, lambda i, m: (0, 0))
     message_shape = (devices, TILE, DH)
-    codes, message = pl.pallas_call(
+    message = pl.pallas_call(
         functools.partial(prepare, pb_count, kv_count, blocks_here),
         grid_spec=pltpu.PrefetchScalarGridSpec(
             num_scalar_prefetch=1,
             grid=(1,),
             in_specs=[held, first, first, last, last],
-            out_specs=[held, pl.BlockSpec(message_shape, lambda i, m: (0, 0, 0))],
+            out_specs=pl.BlockSpec(message_shape, lambda i, m: (0, 0, 0)),
         ),
-        out_shape=[
-            jax.ShapeDtypeStruct(listed.shape, jnp.int32),
-            jax.ShapeDtypeStruct(message_shape, jnp.bfloat16),
-        ],
+        out_shape=jax.ShapeDtypeStruct(message_shape, jnp.bfloat16),
     )(me, listed, keys, values, keys, values)
 
-    held_tiles = pl.pallas_call(
-        stage,
+    listing = pl.BlockSpec(listed.shape, lambda i: (0, 0))
+    held_tiles, codes = pl.pallas_call(
+        functools.partial(stage, pb_count, kv_count, blocks_here),
         grid=(1,),
         in_specs=[
+            listing,
             pl.BlockSpec(keys.shape, lambda i: (0, 0)),
             pl.BlockSpec(values.shape, lambda i: (0, 0)),
         ],
-        out_specs=pl.BlockSpec(memory_space=pltpu.VMEM),
-        out_shape=jax.ShapeDtypeStruct((2,) + keys.shape, keys.dtype),
+        out_specs=[pl.BlockSpec(memory_space=pltpu.VMEM), listing],
+        out_shape=[
+            jax.ShapeDtypeStruct((2,) + keys.shape, keys.dtype),
+            jax.ShapeDtypeStruct(listed.shape, jnp.int32),
+        ],
         compiler_params=pltpu.CompilerParams(vmem_limit_bytes=8 << 20),
-    )(keys, values)
+    )(listed, keys, values)
     answer = exchange(message)
     asked = answer[:, PIECE, :CAP].astype(jnp.int32).reshape(-1)
     parcel_shape = (devices, 2 * CAP * BLOCK + TILE, DH)

time: 88 us -> 88 us (level)
  waiting for transfers between devices: 5.34 us -> 4.45 us
    all_to_all x1, waiting for transfers between devices: 5.34 us -> 4.45 us  [exchange(): return lax.all_to_all(array, ALL, split_axis=0, concat_axis=0, tiled=True)]
where the time goes in v8:
time: 88 us; the launch traced here: 87.6 us
  blocking collectives  53.8 us (61%)
  Pallas kernels  19.1 us (22%)
  starting transfers between devices  7.3 us (8%)
  waiting for transfers between devices  4.45 us (5%)
  local copies, waits for them, and re-layouts  2.88 us (3%)
    all_to_all x1, blocking collectives, exchange(): return lax.all_to_all(array, ALL, split_axis=0, concat_axis=0, tiled=True)  53.8 us
    pallas_call x1, Pallas kernels, per_device(): pl.pallas_call(functools.partial(attend, per_step), out_shape=jax.ShapeDt...  16.4 us
    all_to_all x1, starting transfers between devices, exchange(): return lax.all_to_all(array, ALL, split_axis=0, concat_axis=0, tiled=True)  7.3 us
    all_to_all x1, waiting for transfers between devices, exchange(): return lax.all_to_all(array, ALL, split_axis=0, concat_axis=0, tiled=True)  4.45 us
    unnamed x8, local copies, waits for them, and re-layouts  2.78 us
  transfers between devices with their start and end apart: 1, of which 1 were waited for; matrix products, arithmetic and copies ran while one was open for 0% of the time, Pallas kernels for 0%

profile of v8, /device:TPU:0, one launch (start us, length us, event | category | flops | bytes accessed | tf_op | source)
XLA Modules:
  0.0 87.6 jit_solution(9684985818350927175)
XLA Ops:
  0.0 1.7 %shard_map.47 = bf16[32,8,128]{2,1,0:T(8,128)(2,1)} custom-call(s32[1]{0:T(128)} %bitcast.1.me_ref, s32[14,24]{1,0:T(8,128)} %bitcast.2, bf16[2048,128]{1,0:T(8,128)(2,1)} %lk.1, bf16[2048,128]{1,0:T(8,128)(2,1)} %lv.1, bf16[2048,128]{1,0:T(8,128)(2,1)} %lk.1, bf16[2048,128]{1,0:T(8,128)(2,1)} %lv.1), custom_call_target="tpu_custom_call" | custom-call | tf_op jit(solution)/shard_map/pallas_call | solution.py:206
  1.7 7.3 %all-to-all-start = ((bf16[32,8,128]{2,1,0:T(8,128)(2,1)}), bf16[32,8,128]{2,1,0:T(8,128)(2,1)S(1)}, u32[]{:S(2)}, u32[]{:S(2)}) async-start(bf16[32,8,128]{2,1,0:T(8,128)(2,1)} %shard_map.47), calls=%async_computation | async-start | bytes 131072 | tf_op jit(solution)/shard_map/all_to_all | solution.py:28
  9.0 0.0 copy-start
  9.0 1.0 %copy-done = bf16[2048,128]{1,0:T(8,128)(2,1)S(1)} copy-done((bf16[2048,128]{1,0:T(8,128)(2,1)S(1)}, bf16[2048,128]{1,0:T(8,128)(2,1)}, u32[]{:S(2)}) %copy-start) | copy-done | bytes 524312
  10.0 0.0 copy-start.1
  10.0 1.0 %copy-done.1 = bf16[2048,128]{1,0:T(8,128)(2,1)S(1)} copy-done((bf16[2048,128]{1,0:T(8,128)(2,1)S(1)}, bf16[2048,128]{1,0:T(8,128)(2,1)}, u32[]{:S(2)}) %copy-start.1) | copy-done | bytes 524312
  11.1 0.0 copy-start.3
  11.1 0.7 copy-done.3
  11.8 0.3 shard_map.46
  12.0 4.4 %all-to-all-done.answer_ref = bf16[32,8,128]{2,1,0:T(8,128)(2,1)S(1)} async-done(((bf16[32,8,128]{2,1,0:T(8,128)(2,1)}), bf16[32,8,128]{2,1,0:T(8,128)(2,1)S(1)}, u32[]{:S(2)}, u32[]{:S(2)}) %all-to-all-start) | async-done | bytes 65568 | tf_op jit(solution)/shard_map/all_to_all | solution.py:28
  16.5 0.1 fusion
  16.5 0.1 reshape.4.asked
  16.6 0.0 copy-start.2
  16.7 0.7 shard_map.48
  17.4 53.8 %all_to_all.10.table_ref = bf16[32,264,128]{2,1,0:T(8,128)(2,1)S(1)} all-to-all(bf16[32,264,128]{2,1,0:T(8,128)(2,1)S(1)} %shard_map.48), channel_id=1, replica_groups=mesh['pb'=8,'kv'=4] {'pb','kv'}, dimensions={0} | all-to-all | bytes 4325376 | tf_op jit(solution)/shard_map/all_to_all | solution.py:28
  71.2 0.0 copy-done.2
  71.2 16.4 %shard_map.49 = bf16[1536,1024]{1,0:T(8,128)(2,1)} custom-call(s32[14,24]{1,0:T(8,128)S(1)} %get-tuple-element.7.codes, bf16[1536,1024]{1,0:T(8,128)(2,1)S(1)} %copy-done.2, bf16[32,264,128]{2,1,0:T(8,128)(2,1)S(1)} %all_to_all.10.table_ref), custom_call_target="tpu_custom_call" | custom-call | tf_op jit(solution)/shard_map/pallas_call | solution.py:251
Async XLA Ops:
  1.7 14.8 %all-to-all-start = ((bf16[32,8,128]{2,1,0:T(8,128)(2,1)}), bf16[32,8,128]{2,1,0:T(8,128)(2,1)S(1)}, u32[]{:S(2)}, u32[]{:S(2)}) async-start(bf16[32,8,128]{2,1,0:T(8,128)(2,1)} %shard_map.47), calls=%async_computation | async-start | bytes 131072 | tf_op jit(solution)/shard_map/all_to_all | solution.py:28
  9.0 1.0 %copy-start = (bf16[2048,128]{1,0:T(8,128)(2,1)S(1)}, bf16[2048,128]{1,0:T(8,128)(2,1)}, u32[]{:S(2)}) copy-start(bf16[2048,128]{1,0:T(8,128)(2,1)} %lk.1) | copy-start | bytes 1572868
  10.0 1.0 %copy-start.1 = (bf16[2048,128]{1,0:T(8,128)(2,1)S(1)}, bf16[2048,128]{1,0:T(8,128)(2,1)}, u32[]{:S(2)}) copy-start(bf16[2048,128]{1,0:T(8,128)(2,1)} %lv.1) | copy-start | bytes 1572868
  11.1 0.7 copy-start.3
  16.6 54.6 %copy-start.2 = (bf16[1536,1024]{1,0:T(8,128)(2,1)S(1)}, bf16[1536,1024]{1,0:T(8,128)(2,1)}, u32[]{:S(2)}) copy-start(bf16[1536,1024]{1,0:T(8,128)(2,1)} %q_ref.1) | copy-start | bytes 9437188

commit v9 on v8

--- a/solution.py
+++ b/solution.py
@@ -57,14 +57,12 @@
     return place, local, ids, low, high
 
 
-def prepare(pb_count, kv_count, blocks_here, me_ref, selected_ref, fk, fv, lk, lv, message_ref):
+def prepare(pb_count, kv_count, blocks_here, me_ref, selected_ref, edge_k, edge_v, message_ref):
     devices = pb_count * kv_count
     low, high = wanted(pb_count, kv_count, blocks_here, selected_ref)[3:]
     lane = lax.broadcasted_iota(jnp.int32, (devices, DH), 1)
     wants = jnp.where(lane == 0, low, jnp.where(lane == 1, high, 0)).astype(jnp.float32)
-    first = me_ref[0] == 0
-    edge = jnp.concatenate([jnp.where(first, fk[...], lk[...]), jnp.where(first, fv[...], lv[...])], axis=0)
-    edge = edge.astype(jnp.float32)
+    edge = jnp.concatenate([edge_k[...], edge_v[...]], axis=0).astype(jnp.float32)
     upper = lax.broadcasted_iota(jnp.int32, (TILE, DH), 0) < PIECE
     for m in range(devices):
         at = m % PIECES // 2 * TILE
@@ -88,7 +86,7 @@
     last = answer_ref[devices - 1].astype(jnp.float32)
     piece = jnp.concatenate([first[:PIECE], last[:PIECE]], axis=0).astype(jnp.bfloat16)
 
-    @pl.loop(0, devices, unroll=4)
+    @pl.loop(0, devices, unroll=8)
     def _(m):
         for slot in range(CAP):
             row = pl.multiple_of(asked[m * CAP + slot] * BLOCK, BLOCK)
@@ -160,7 +158,7 @@
         total = product if g == 0 else total + product
         if g == groups - 1:
             sums = total[:, DH:]
-            parts = [sums[i * 8 : (i + 1) * 8] for i in range(CHUNK // 8)]
+            parts = [sums[i * 32 : (i + 1) * 32] for i in range(CHUNK // 32)]
             largest = functools.reduce(jnp.maximum, parts if largest is None else [largest, *parts])
             store(n, c, total)
 
@@ -199,8 +197,7 @@
 
     listed = selected.T
     me = lax.axis_index(ALL).astype(jnp.int32)[None]
-    first = pl.BlockSpec((BLOCK, DH), lambda i, m: (0, 0))
-    last = pl.BlockSpec((BLOCK, DH), lambda i, m: (blocks_here - 1, 0))
+    edge = pl.BlockSpec((BLOCK, DH), lambda i, m: (jnp.where(m[0] == 0, 0, blocks_here - 1), 0))
     held = pl.BlockSpec(listed.shape, lambda i, m: (0, 0))
     message_shape = (devices, TILE, DH)
     message = pl.pallas_call(
@@ -208,11 +205,11 @@
         grid_spec=pltpu.PrefetchScalarGridSpec(
             num_scalar_prefetch=1,
             grid=(1,),
-            in_specs=[held, first, first, last, last],
+            in_specs=[held, edge, edge],
             out_specs=pl.BlockSpec(message_shape, lambda i, m: (0, 0, 0)),
         ),
         out_shape=jax.ShapeDtypeStruct(message_shape, jnp.bfloat16),
-    )(me, listed, keys, values, keys, values)
+    )(me, listed, keys, values)
 
     listing = pl.BlockSpec(listed.shape, lambda i: (0, 0))
     held_tiles, codes = pl.pallas_call(

time: 88 us -> 87.9 us (level)
  no operation moved by 1% of the time
where the time goes in v9:
time: 87.9 us; the launch traced here: 87.5 us
  blocking collectives  53.8 us (61%)
  Pallas kernels  19 us (22%)
  starting transfers between devices  7.3 us (8%)
  waiting for transfers between devices  4.45 us (5%)
  local copies, waits for them, and re-layouts  2.88 us (3%)
    all_to_all x1, blocking collectives, exchange(): return lax.all_to_all(array, ALL, split_axis=0, concat_axis=0, tiled=True)  53.8 us
    pallas_call x1, Pallas kernels, per_device(): pl.pallas_call(functools.partial(attend, per_step), out_shape=jax.ShapeDt...  16.4 us
    all_to_all x1, starting transfers between devices, exchange(): return lax.all_to_all(array, ALL, split_axis=0, concat_axis=0, tiled=True)  7.3 us
    all_to_all x1, waiting for transfers between devices, exchange(): return lax.all_to_all(array, ALL, split_axis=0, concat_axis=0, tiled=True)  4.45 us
    unnamed x8, local copies, waits for them, and re-layouts  2.78 us
  transfers between devices with their start and end apart: 1, of which 1 were waited for; matrix products, arithmetic and copies ran while one was open for 0% of the time, Pallas kernels for 0%

profile of v9, /device:TPU:0, one launch (start us, length us, event | category | flops | bytes accessed | tf_op | source)
XLA Modules:
  0.0 87.5 jit_solution(4706505194528336623)
XLA Ops:
  0.0 1.6 %shard_map.47 = bf16[32,8,128]{2,1,0:T(8,128)(2,1)} custom-call(s32[1]{0:T(128)} %bitcast.1.me_ref, s32[14,24]{1,0:T(8,128)} %bitcast.2, bf16[2048,128]{1,0:T(8,128)(2,1)} %edge_k.1, bf16[2048,128]{1,0:T(8,128)(2,1)} %edge_v.1), custom_call_target="tpu_custom_call" | custom-call | tf_op jit(solution)/shard_map/pallas_call | solution.py:203
  1.6 7.3 %all-to-all-start = ((bf16[32,8,128]{2,1,0:T(8,128)(2,1)}), bf16[32,8,128]{2,1,0:T(8,128)(2,1)S(1)}, u32[]{:S(2)}, u32[]{:S(2)}) async-start(bf16[32,8,128]{2,1,0:T(8,128)(2,1)} %shard_map.47), calls=%async_computation | async-start | bytes 131072 | tf_op jit(solution)/shard_map/all_to_all | solution.py:28
  8.9 0.0 copy-start.1
  8.9 1.0 %copy-done.1 = bf16[2048,128]{1,0:T(8,128)(2,1)S(1)} copy-done((bf16[2048,128]{1,0:T(8,128)(2,1)S(1)}, bf16[2048,128]{1,0:T(8,128)(2,1)}, u32[]{:S(2)}) %copy-start.1) | copy-done | bytes 524312
  10.0 0.0 copy-start.2
  10.0 1.0 %copy-done.2 = bf16[2048,128]{1,0:T(8,128)(2,1)S(1)} copy-done((bf16[2048,128]{1,0:T(8,128)(2,1)S(1)}, bf16[2048,128]{1,0:T(8,128)(2,1)}, u32[]{:S(2)}) %copy-start.2) | copy-done | bytes 524312
  11.0 0.0 copy-start.3
  11.0 0.7 copy-done.3
  11.7 0.3 shard_map.46
  12.0 4.4 %all-to-all-done.answer_ref = bf16[32,8,128]{2,1,0:T(8,128)(2,1)S(1)} async-done(((bf16[32,8,128]{2,1,0:T(8,128)(2,1)}), bf16[32,8,128]{2,1,0:T(8,128)(2,1)S(1)}, u32[]{:S(2)}, u32[]{:S(2)}) %all-to-all-start) | async-done | bytes 65568 | tf_op jit(solution)/shard_map/all_to_all | solution.py:28
  16.4 0.1 fusion
  16.5 0.1 reshape.4.asked
  16.6 0.0 copy-start
  16.6 0.7 shard_map.48
  17.3 53.8 %all_to_all.10.table_ref = bf16[32,264,128]{2,1,0:T(8,128)(2,1)S(1)} all-to-all(bf16[32,264,128]{2,1,0:T(8,128)(2,1)S(1)} %shard_map.48), channel_id=1, replica_groups=mesh['pb'=8,'kv'=4] {'pb','kv'}, dimensions={0} | all-to-all | bytes 4325376 | tf_op jit(solution)/shard_map/all_to_all | solution.py:28
  71.1 0.0 copy-done
  71.1 16.4 %shard_map.49 = bf16[1536,1024]{1,0:T(8,128)(2,1)} custom-call(s32[14,24]{1,0:T(8,128)S(1)} %get-tuple-element.7.codes, bf16[1536,1024]{1,0:T(8,128)(2,1)S(1)} %copy-done, bf16[32,264,128]{2,1,0:T(8,128)(2,1)S(1)} %all_to_all.10.table_ref), custom_call_target="tpu_custom_call" | custom-call | tf_op jit(solution)/shard_map/pallas_call | solution.py:248
Async XLA Ops:
  1.6 14.8 %all-to-all-start = ((bf16[32,8,128]{2,1,0:T(8,128)(2,1)}), bf16[32,8,128]{2,1,0:T(8,128)(2,1)S(1)}, u32[]{:S(2)}, u32[]{:S(2)}) async-start(bf16[32,8,128]{2,1,0:T(8,128)(2,1)} %shard_map.47), calls=%async_computation | async-start | bytes 131072 | tf_op jit(solution)/shard_map/all_to_all | solution.py:28
  8.9 1.0 %copy-start.1 = (bf16[2048,128]{1,0:T(8,128)(2,1)S(1)}, bf16[2048,128]{1,0:T(8,128)(2,1)}, u32[]{:S(2)}) copy-start(bf16[2048,128]{1,0:T(8,128)(2,1)} %edge_k.1) | copy-start | bytes 1572868
  10.0 1.0 %copy-start.2 = (bf16[2048,128]{1,0:T(8,128)(2,1)S(1)}, bf16[2048,128]{1,0:T(8,128)(2,1)}, u32[]{:S(2)}) copy-start(bf16[2048,128]{1,0:T(8,128)(2,1)} %edge_v.1) | copy-start | bytes 1572868
  11.0 0.7 copy-start.3
  16.6 54.5 %copy-start = (bf16[1536,1024]{1,0:T(8,128)(2,1)S(1)}, bf16[1536,1024]{1,0:T(8,128)(2,1)}, u32[]{:S(2)}) copy-start(bf16[1536,1024]{1,0:T(8,128)(2,1)} %q_ref.1) | copy-start | bytes 9437188

commit v10 on v9

--- a/solution.py
+++ b/solution.py
@@ -18,7 +18,7 @@
 PIECE = 2 * BLOCK // PIECES
 TILE = 2 * PIECE
 CHUNK = 256
-GROUP = 4
+GROUP = 8
 TRUSTED = 2.0 ** 100
 SCALE = DH ** -0.5 * math.log2(math.e)
 ALL = ("pb", "kv")

time: 87.9 us -> 88.2 us (level)
  no operation moved by 1% of the time
where the time goes in v10:
time: 88.2 us; the launch traced here: 87.8 us
  blocking collectives  53.8 us (61%)
  Pallas kernels  19.3 us (22%)
  starting transfers between devices  7.3 us (8%)
  waiting for transfers between devices  4.45 us (5%)
  local copies, waits for them, and re-layouts  2.88 us (3%)
    all_to_all x1, blocking collectives, exchange(): return lax.all_to_all(array, ALL, split_axis=0, concat_axis=0, tiled=True)  53.8 us
    pallas_call x1, Pallas kernels, per_device(): pl.pallas_call(functools.partial(attend, per_step), out_shape=jax.ShapeDt...  16.7 us
    all_to_all x1, starting transfers between devices, exchange(): return lax.all_to_all(array, ALL, split_axis=0, concat_axis=0, tiled=True)  7.3 us
    all_to_all x1, waiting for transfers between devices, exchange(): return lax.all_to_all(array, ALL, split_axis=0, concat_axis=0, tiled=True)  4.45 us
    unnamed x8, local copies, waits for them, and re-layouts  2.78 us
  transfers between devices with their start and end apart: 1, of which 1 were waited for; matrix products, arithmetic and copies ran while one was open for 0% of the time, Pallas kernels for 0%

profile of v10, /device:TPU:0, one launch (start us, length us, event | category | flops | bytes accessed | tf_op | source)
XLA Modules:
  0.0 87.8 jit_solution(10561620370309506649)
XLA Ops:
  0.0 1.6 %shard_map.47 = bf16[32,8,128]{2,1,0:T(8,128)(2,1)} custom-call(s32[1]{0:T(128)} %bitcast.1.me_ref, s32[14,24]{1,0:T(8,128)} %bitcast.2, bf16[2048,128]{1,0:T(8,128)(2,1)} %edge_k.1, bf16[2048,128]{1,0:T(8,128)(2,1)} %edge_v.1), custom_call_target="tpu_custom_call" | custom-call | tf_op jit(solution)/shard_map/pallas_call | solution.py:203
  1.6 7.3 %all-to-all-start = ((bf16[32,8,128]{2,1,0:T(8,128)(2,1)}), bf16[32,8,128]{2,1,0:T(8,128)(2,1)S(1)}, u32[]{:S(2)}, u32[]{:S(2)}) async-start(bf16[32,8,128]{2,1,0:T(8,128)(2,1)} %shard_map.47), calls=%async_computation | async-start | bytes 131072 | tf_op jit(solution)/shard_map/all_to_all | solution.py:28
  8.9 0.0 copy-start.1
  8.9 1.0 %copy-done.1 = bf16[2048,128]{1,0:T(8,128)(2,1)S(1)} copy-done((bf16[2048,128]{1,0:T(8,128)(2,1)S(1)}, bf16[2048,128]{1,0:T(8,128)(2,1)}, u32[]{:S(2)}) %copy-start.1) | copy-done | bytes 524312
  10.0 0.0 copy-start.2
  10.0 1.0 %copy-done.2 = bf16[2048,128]{1,0:T(8,128)(2,1)S(1)} copy-done((bf16[2048,128]{1,0:T(8,128)(2,1)S(1)}, bf16[2048,128]{1,0:T(8,128)(2,1)}, u32[]{:S(2)}) %copy-start.2) | copy-done | bytes 524312
  11.0 0.0 copy-start.3
  11.0 0.7 copy-done.3
  11.7 0.3 shard_map.46
  12.0 4.4 %all-to-all-done.answer_ref = bf16[32,8,128]{2,1,0:T(8,128)(2,1)S(1)} async-done(((bf16[32,8,128]{2,1,0:T(8,128)(2,1)}), bf16[32,8,128]{2,1,0:T(8,128)(2,1)S(1)}, u32[]{:S(2)}, u32[]{:S(2)}) %all-to-all-start) | async-done | bytes 65568 | tf_op jit(solution)/shard_map/all_to_all | solution.py:28
  16.4 0.1 fusion
  16.5 0.1 reshape.4.asked
  16.6 0.0 copy-start
  16.6 0.7 shard_map.48
  17.3 53.8 %all_to_all.10.table_ref = bf16[32,264,128]{2,1,0:T(8,128)(2,1)S(1)} all-to-all(bf16[32,264,128]{2,1,0:T(8,128)(2,1)S(1)} %shard_map.48), channel_id=1, replica_groups=mesh['pb'=8,'kv'=4] {'pb','kv'}, dimensions={0} | all-to-all | bytes 4325376 | tf_op jit(solution)/shard_map/all_to_all | solution.py:28
  71.1 0.0 copy-done
  71.1 16.7 %shard_map.49 = bf16[1536,1024]{1,0:T(8,128)(2,1)} custom-call(s32[14,24]{1,0:T(8,128)S(1)} %get-tuple-element.7.codes, bf16[1536,1024]{1,0:T(8,128)(2,1)S(1)} %copy-done, bf16[32,264,128]{2,1,0:T(8,128)(2,1)S(1)} %all_to_all.10.table_ref), custom_call_target="tpu_custom_call" | custom-call | tf_op jit(solution)/shard_map/pallas_call | solution.py:248
Async XLA Ops:
  1.6 14.8 %all-to-all-start = ((bf16[32,8,128]{2,1,0:T(8,128)(2,1)}), bf16[32,8,128]{2,1,0:T(8,128)(2,1)S(1)}, u32[]{:S(2)}, u32[]{:S(2)}) async-start(bf16[32,8,128]{2,1,0:T(8,128)(2,1)} %shard_map.47), calls=%async_computation | async-start | bytes 131072 | tf_op jit(solution)/shard_map/all_to_all | solution.py:28
  8.9 1.0 %copy-start.1 = (bf16[2048,128]{1,0:T(8,128)(2,1)S(1)}, bf16[2048,128]{1,0:T(8,128)(2,1)}, u32[]{:S(2)}) copy-start(bf16[2048,128]{1,0:T(8,128)(2,1)} %edge_k.1) | copy-start | bytes 1572868
  10.0 1.0 %copy-start.2 = (bf16[2048,128]{1,0:T(8,128)(2,1)S(1)}, bf16[2048,128]{1,0:T(8,128)(2,1)}, u32[]{:S(2)}) copy-start(bf16[2048,128]{1,0:T(8,128)(2,1)} %edge_v.1) | copy-start | bytes 1572868
  11.0 0.7 copy-start.3
  16.6 54.5 %copy-start = (bf16[1536,1024]{1,0:T(8,128)(2,1)S(1)}, bf16[1536,1024]{1,0:T(8,128)(2,1)}, u32[]{:S(2)}) copy-start(bf16[1536,1024]{1,0:T(8,128)(2,1)} %q_ref.1) | copy-start | bytes 9437188

commit v11 on v9

--- a/solution.py
+++ b/solution.py
@@ -206,7 +206,7 @@
             num_scalar_prefetch=1,
             grid=(1,),
             in_specs=[held, edge, edge],
-            out_specs=pl.BlockSpec(message_shape, lambda i, m: (0, 0, 0)),
+            out_specs=pl.BlockSpec(memory_space=pltpu.VMEM),
         ),
         out_shape=jax.ShapeDtypeStruct(message_shape, jnp.bfloat16),
     )(me, listed, keys, values)

time: 87.9 us -> 87.9 us (level)
  no operation moved by 1% of the time
where the time goes in v11:
time: 87.9 us; the launch traced here: 87.5 us
  blocking collectives  53.8 us (61%)
  Pallas kernels  19 us (22%)
  starting transfers between devices  7.3 us (8%)
  waiting for transfers between devices  4.45 us (5%)
  local copies, waits for them, and re-layouts  2.88 us (3%)
    all_to_all x1, blocking collectives, exchange(): return lax.all_to_all(array, ALL, split_axis=0, concat_axis=0, tiled=True)  53.8 us
    pallas_call x1, Pallas kernels, per_device(): pl.pallas_call(functools.partial(attend, per_step), out_shape=jax.ShapeDt...  16.4 us
    all_to_all x1, starting transfers between devices, exchange(): return lax.all_to_all(array, ALL, split_axis=0, concat_axis=0, tiled=True)  7.3 us
    all_to_all x1, waiting for transfers between devices, exchange(): return lax.all_to_all(array, ALL, split_axis=0, concat_axis=0, tiled=True)  4.45 us
    unnamed x8, local copies, waits for them, and re-layouts  2.78 us
  transfers between devices with their start and end apart: 1, of which 1 were waited for; matrix products, arithmetic and copies ran while one was open for 0% of the time, Pallas kernels for 0%

profile of v11, /device:TPU:0, one launch (start us, length us, event | category | flops | bytes accessed | tf_op | source)
XLA Modules:
  0.0 87.5 jit_solution(4706505194528336623)
XLA Ops:
  0.0 1.6 %shard_map.47 = bf16[32,8,128]{2,1,0:T(8,128)(2,1)} custom-call(s32[1]{0:T(128)} %bitcast.1.me_ref, s32[14,24]{1,0:T(8,128)} %bitcast.2, bf16[2048,128]{1,0:T(8,128)(2,1)} %edge_k.1, bf16[2048,128]{1,0:T(8,128)(2,1)} %edge_v.1), custom_call_target="tpu_custom_call" | custom-call | tf_op jit(solution)/shard_map/pallas_call | solution.py:203
  1.6 7.3 %all-to-all-start = ((bf16[32,8,128]{2,1,0:T(8,128)(2,1)}), bf16[32,8,128]{2,1,0:T(8,128)(2,1)S(1)}, u32[]{:S(2)}, u32[]{:S(2)}) async-start(bf16[32,8,128]{2,1,0:T(8,128)(2,1)} %shard_map.47), calls=%async_computation | async-start | bytes 131072 | tf_op jit(solution)/shard_map/all_to_all | solution.py:28
  8.9 0.0 copy-start.1
  8.9 1.0 %copy-done.1 = bf16[2048,128]{1,0:T(8,128)(2,1)S(1)} copy-done((bf16[2048,128]{1,0:T(8,128)(2,1)S(1)}, bf16[2048,128]{1,0:T(8,128)(2,1)}, u32[]{:S(2)}) %copy-start.1) | copy-done | bytes 524312
  10.0 0.0 copy-start.2
  10.0 1.0 %copy-done.2 = bf16[2048,128]{1,0:T(8,128)(2,1)S(1)} copy-done((bf16[2048,128]{1,0:T(8,128)(2,1)S(1)}, bf16[2048,128]{1,0:T(8,128)(2,1)}, u32[]{:S(2)}) %copy-start.2) | copy-done | bytes 524312
  11.0 0.0 copy-start.3
  11.0 0.7 copy-done.3
  11.7 0.3 shard_map.46
  12.0 4.4 %all-to-all-done.answer_ref = bf16[32,8,128]{2,1,0:T(8,128)(2,1)S(1)} async-done(((bf16[32,8,128]{2,1,0:T(8,128)(2,1)}), bf16[32,8,128]{2,1,0:T(8,128)(2,1)S(1)}, u32[]{:S(2)}, u32[]{:S(2)}) %all-to-all-start) | async-done | bytes 65568 | tf_op jit(solution)/shard_map/all_to_all | solution.py:28
  16.4 0.1 fusion
  16.5 0.1 reshape.4.asked
  16.6 0.0 copy-start
  16.6 0.7 shard_map.48
  17.3 53.8 %all_to_all.10.table_ref = bf16[32,264,128]{2,1,0:T(8,128)(2,1)S(1)} all-to-all(bf16[32,264,128]{2,1,0:T(8,128)(2,1)S(1)} %shard_map.48), channel_id=1, replica_groups=mesh['pb'=8,'kv'=4] {'pb','kv'}, dimensions={0} | all-to-all | bytes 4325376 | tf_op jit(solution)/shard_map/all_to_all | solution.py:28
  71.1 0.0 copy-done
  71.1 16.4 %shard_map.49 = bf16[1536,1024]{1,0:T(8,128)(2,1)} custom-call(s32[14,24]{1,0:T(8,128)S(1)} %get-tuple-element.7.codes, bf16[1536,1024]{1,0:T(8,128)(2,1)S(1)} %copy-done, bf16[32,264,128]{2,1,0:T(8,128)(2,1)S(1)} %all_to_all.10.table_ref), custom_call_target="tpu_custom_call" | custom-call | tf_op jit(solution)/shard_map/pallas_call | solution.py:248
Async XLA Ops:
  1.6 14.8 %all-to-all-start = ((bf16[32,8,128]{2,1,0:T(8,128)(2,1)}), bf16[32,8,128]{2,1,0:T(8,128)(2,1)S(1)}, u32[]{:S(2)}, u32[]{:S(2)}) async-start(bf16[32,8,128]{2,1,0:T(8,128)(2,1)} %shard_map.47), calls=%async_computation | async-start | bytes 131072 | tf_op jit(solution)/shard_map/all_to_all | solution.py:28
  8.9 1.0 %copy-start.1 = (bf16[2048,128]{1,0:T(8,128)(2,1)S(1)}, bf16[2048,128]{1,0:T(8,128)(2,1)}, u32[]{:S(2)}) copy-start(bf16[2048,128]{1,0:T(8,128)(2,1)} %edge_k.1) | copy-start | bytes 1572868
  10.0 1.0 %copy-start.2 = (bf16[2048,128]{1,0:T(8,128)(2,1)S(1)}, bf16[2048,128]{1,0:T(8,128)(2,1)}, u32[]{:S(2)}) copy-start(bf16[2048,128]{1,0:T(8,128)(2,1)} %edge_v.1) | copy-start | bytes 1572868
  11.0 0.7 copy-start.3
  16.6 54.5 %copy-start = (bf16[1536,1024]{1,0:T(8,128)(2,1)S(1)}, bf16[1536,1024]{1,0:T(8,128)(2,1)}, u32[]{:S(2)}) copy-start(bf16[1536,1024]{1,0:T(8,128)(2,1)} %q_ref.1) | copy-start | bytes 9437188
